TPU v7x, 32 devices: a whole 2x2x4 slice. The times are simulated.
32 devices in a mesh: dp: 4 (over z), space: 8 (over y, x, core).
Axes of the slice: x: 2, y: 2, z: 4, core: 2. Of those that a mesh axis runs over, the one named last changes fastest.
Arguments:
- features: bfloat16 [4, 24, 64, 1024], P('dp', 'space'), may hold values from -6 to 6
- cotangent: bfloat16 [4, 24, 128, 128], P('dp', 'space'), may hold values from -6 to 6
- conv_one: bfloat16 [64, 1728], P('dp'), may hold values from -0.15625 to 0.15625
- down_weight: bfloat16 [128, 512], P('dp'), may hold values from -0.25 to 0.25
- conv_two: bfloat16 [128, 3456], P('dp'), may hold values from -0.109375 to 0.109375
- patch_home: int32 [16], replicated, may hold values from 0 to 23, as said below
- patch_links: int32 [16, 4], replicated, may hold values from -1 to 15, as said below
Outputs:
- level_two: bfloat16 [4, 24, 128, 128], P('dp', 'space')
- grad_conv_one: float32 [64, 1728], P('dp')
- grad_conv_down: float32 [128, 512], P('dp')
- grad_conv_two: float32 [128, 3456], P('dp')
Inputs may be any that keep to these rules, and one draw needn't show every extreme that they name: Patch p sits on device patch_home[p] // 3 of the space axis in slot patch_home[p] % 3; no two patches share a slot; every device holds a run of consecutive patch numbers, the runs in the order of the devices, each of 1 to 3 patches; some device holds exactly 3 and some exactly one. `patch_links`: the patches form a grid of 2 columns and 8 rows, patch 2 r + c in row r and column c; the four entries of a patch name p - 1, p + 1, p - 2, p + 2 or -1 where the grid ends or the link is cut; links are symmetric; the first and the last row are linked across x.
All inputs are finite; a program needn't handle non-finite values.
Results may differ from a plain program's by a relative error of at most 0.014.
Values may be sent and summed in bfloat16 or wider, within the bound.
A program may use at most 128 MiB of HBM per device.

v0:
```python
import jax
import jax.numpy as jnp
from jax import lax
from jax.sharding import PartitionSpec as P

PXY = 16
PZ = 4


def shifted(value, axis, by):
    size = lax.axis_size(axis)
    pairs = [(i, i + by) for i in range(size) if 0 <= i + by < size]
    return lax.ppermute(value, axis, pairs)


def silu_slope(values):
    logistic = jax.nn.sigmoid(values)
    return logistic * (1.0 + values * (1.0 - logistic))


def slot_table(owners, linkage, target, first_side, slot_count):
    patches = owners.shape[0]
    slot_codes = target * slot_count + jnp.arange(slot_count, dtype=jnp.int32)
    matches = owners[None, :] == slot_codes[:, None]
    living = jnp.any(matches, axis=1)
    patch_ids = jnp.sum(
        jnp.where(matches, jnp.arange(patches, dtype=jnp.int32)[None, :], 0), axis=1
    )
    linked = jnp.take(linkage, patch_ids, axis=0)[:, first_side : first_side + 2]
    usable = living[:, None] & (linked >= 0)
    sources = jnp.take(owners, jnp.maximum(linked, 0), axis=0)
    return (usable, sources // slot_count, sources % slot_count, living)


def outgoing(face_set, owners, linkage, my_index, offset, first_side):
    slot_count = face_set.shape[0]
    usable, source_dev, source_slot, living = slot_table(
        owners, linkage, my_index + offset, first_side, slot_count
    )
    flipped = face_set[:, ::-1].reshape((slot_count * 2,) + face_set.shape[2:])
    take_at = source_slot * 2 + jnp.arange(2, dtype=jnp.int32)[None, :]
    picked = jnp.take(flipped, take_at.reshape(-1), axis=0).reshape(face_set.shape)
    wanted = usable & (source_dev == my_index)
    return jnp.where(wanted[:, :, None, None], picked, jnp.zeros_like(picked))


def halo_section(face_set, owners, linkage, my_index, first_side, reach_devs):
    slot_count = face_set.shape[0]
    usable, source_dev, source_slot, living = slot_table(
        owners, linkage, my_index, first_side, slot_count
    )
    rim_faces = jnp.zeros_like(face_set)
    for offset in range(-reach_devs, reach_devs + 1):
        chosen = usable & (source_dev == my_index - offset)
        if offset == 0:
            parcel = outgoing(face_set, owners, linkage, my_index, 0, first_side)
            rim_faces = jnp.where(chosen[:, :, None, None], parcel, rim_faces)
        else:
            parcel = outgoing(face_set, owners, linkage, my_index, offset, first_side)
            parcel = shifted(parcel, "space", offset)
            rim_faces = jnp.where(chosen[:, :, None, None], parcel, rim_faces)
    return rim_faces


def return_section(rim_grads, owners, linkage, my_index, first_side, reach_devs):
    slot_count = rim_grads.shape[0]
    usable, source_dev, source_slot, living = slot_table(
        owners, linkage, my_index, first_side, slot_count
    )
    totals = jnp.zeros_like(rim_grads)
    for offset in range(-reach_devs, reach_devs + 1):
        chosen = usable & (source_dev == my_index - offset)
        portion = jnp.where(chosen[:, :, None, None], rim_grads, jnp.zeros_like(rim_grads))
        if offset != 0:
            portion = shifted(portion.astype(jnp.bfloat16), "space", -offset).astype(portion.dtype)
        sender_ok, target_dev, target_slot, unused = slot_table(
            owners, linkage, my_index + offset, first_side, slot_count
        )
        wanted = sender_ok & (target_dev == my_index)
        one_hot = (
            wanted[:, :, None]
            & (target_slot[:, :, None] == jnp.arange(slot_count, dtype=jnp.int32)[None, None, :])
        ).astype(jnp.float32)
        totals = totals + jnp.einsum(
            "sit,sicm->ticm", one_hot, portion, precision=lax.Precision.HIGHEST
        )
    return totals[:, ::-1]


def assemble(field, owners, linkage, my_index):
    slot_count, channels, size_x, size_y, size_z = field.shape
    along_x = jnp.stack([field[:, :, 0], field[:, :, -1]], axis=1).reshape(
        slot_count, 2, channels, size_y * size_z
    )
    rim_x = halo_section(along_x, owners, linkage, my_index, 0, 1).reshape(
        slot_count, 2, channels, size_y, size_z
    )
    widened = jnp.concatenate([rim_x[:, 0][:, :, None], field, rim_x[:, 1][:, :, None]], axis=2)
    along_y = jnp.stack([widened[:, :, :, 0], widened[:, :, :, -1]], axis=1).reshape(
        slot_count, 2, channels, (size_x + 2) * size_z
    )
    rim_y = halo_section(along_y, owners, linkage, my_index, 2, 2).reshape(
        slot_count, 2, channels, size_x + 2, size_z
    )
    full_block = jnp.concatenate(
        [rim_y[:, 0][:, :, :, None], widened, rim_y[:, 1][:, :, :, None]], axis=3
    )
    return jnp.pad(full_block, ((0, 0), (0, 0), (0, 0), (0, 0), (1, 1)))


def disassemble(grad_padded, owners, linkage, my_index):
    interior = grad_padded[:, :, :, :, 1:-1]
    slot_count, channels, wide_x, wide_y, size_z = interior.shape
    along_y = jnp.stack([interior[:, :, :, 0], interior[:, :, :, -1]], axis=1).reshape(
        slot_count, 2, channels, wide_x * size_z
    )
    back_y = return_section(along_y, owners, linkage, my_index, 2, 2).reshape(
        slot_count, 2, channels, wide_x, size_z
    )
    widened = interior[:, :, :, 1:-1]
    widened = widened.at[:, :, :, 0].add(back_y[:, 0]).at[:, :, :, -1].add(back_y[:, 1])
    along_x = jnp.stack([widened[:, :, 0], widened[:, :, -1]], axis=1).reshape(
        slot_count, 2, channels, (wide_y - 2) * size_z
    )
    back_x = return_section(along_x, owners, linkage, my_index, 0, 1).reshape(
        slot_count, 2, channels, wide_y - 2, size_z
    )
    center_part = widened[:, :, 1:-1]
    return center_part.at[:, :, 0].add(back_x[:, 0]).at[:, :, -1].add(back_x[:, 1])


def tap_stack(padded):
    slot_count, channels, wide_x, wide_y, wide_z = padded.shape
    plane_len = wide_y * wide_z
    length = (wide_y - 2) * wide_z
    flat_plane = jnp.pad(
        padded.reshape(slot_count, channels, wide_x, plane_len), ((0, 0), (0, 0), (0, 0), (1, 1))
    )
    pieces = []
    for shift_y in (-1, 0, 1):
        for shift_z in (-1, 0, 1):
            offset_at = 1 + wide_z + shift_y * wide_z + shift_z
            pieces.append(flat_plane[:, :, :, offset_at : offset_at + length])
    return jnp.stack(pieces, axis=1)


def conv_forward(stacked, kernel_weight, size_x):
    kernel = kernel_weight.reshape(kernel_weight.shape[0], 3, 9, stacked.shape[2])
    summed = jnp.einsum(
        "otc,stcxj->soxj",
        kernel[:, 0],
        stacked[:, :, :, 0:size_x],
        preferred_element_type=jnp.float32,
    )
    for shift_x in (1, 2):
        summed = summed + jnp.einsum(
            "otc,stcxj->soxj",
            kernel[:, shift_x],
            stacked[:, :, :, shift_x : shift_x + size_x],
            preferred_element_type=jnp.float32,
        )
    return summed


def trim(result, size_y, size_z):
    slot_count, channels, size_x, length = result.shape
    return result.reshape(slot_count, channels, size_x, size_y, size_z + 2)[..., 1 : size_z + 1]


def extend(grad_cells):
    slot_count, channels, size_x, size_y, size_z = grad_cells.shape
    widened = jnp.pad(grad_cells, ((0, 0), (0, 0), (0, 0), (0, 0), (1, 1)))
    return widened.reshape(slot_count, channels, size_x, size_y * (size_z + 2))


def weight_grad(stacked, grad_ext, size_x):
    parts_list = []
    for shift_x in range(3):
        parts_list.append(
            jnp.einsum(
                "soxj,stcxj->otc",
                grad_ext,
                stacked[:, :, :, shift_x : shift_x + size_x],
                preferred_element_type=jnp.float32,
            )
        )
    joined = jnp.stack(parts_list, axis=1)
    return joined.reshape(joined.shape[0], 27 * joined.shape[3])


def input_grad(grad_ext, kernel_weight, padded_shape):
    slot_count, channels, wide_x, wide_y, wide_z = padded_shape
    plane_len = wide_y * wide_z
    length = (wide_y - 2) * wide_z
    kernel = kernel_weight.reshape(kernel_weight.shape[0], 3, 9, channels)
    summed = jnp.zeros((slot_count, channels, wide_x, plane_len + 2), jnp.float32)
    for shift_x in range(3):
        spread = jnp.einsum(
            "otc,soxj->stcxj", kernel[:, shift_x], grad_ext, preferred_element_type=jnp.float32
        )
        for tap_index in range(9):
            offset_at = 1 + wide_z + (tap_index // 3 - 1) * wide_z + (tap_index % 3 - 1)
            summed = summed + jnp.pad(
                spread[:, tap_index],
                (
                    (0, 0),
                    (0, 0),
                    (shift_x, 2 - shift_x),
                    (offset_at, plane_len + 2 - offset_at - length),
                ),
            )
    return summed[:, :, :, 1 : plane_len + 1].reshape(padded_shape)


def down_forward(hidden_state, kernel_weight):
    slot_count, channels, size_x, size_y, size_z = hidden_state.shape
    kernel = kernel_weight.reshape(kernel_weight.shape[0], 2, 2, 2, channels)
    blocks = hidden_state.reshape(
        slot_count, channels, size_x // 2, 2, size_y // 2, 2, size_z // 2, 2
    )
    return jnp.einsum("oabcm,smxaybzc->soxyz", kernel, blocks, preferred_element_type=jnp.float32)


def down_backward(hidden_state, kernel_weight, grad_reduced):
    slot_count, channels, size_x, size_y, size_z = hidden_state.shape
    kernel = kernel_weight.reshape(kernel_weight.shape[0], 2, 2, 2, channels)
    blocks = hidden_state.reshape(
        slot_count, channels, size_x // 2, 2, size_y // 2, 2, size_z // 2, 2
    )
    dw_down = jnp.einsum(
        "soxyz,smxaybzc->oabcm", grad_reduced, blocks, preferred_element_type=jnp.float32
    )
    grad_blocks = jnp.einsum(
        "oabcm,soxyz->smxaybzc", kernel, grad_reduced, preferred_element_type=jnp.float32
    )
    return (dw_down.reshape(kernel_weight.shape), grad_blocks.reshape(hidden_state.shape))


def on_device(features, cotangent, conv_one, down_weight, conv_two, patch_home, patch_links):
    full_one, full_down, full_two = (
        lax.all_gather(conv_one, "dp", axis=0, tiled=True),
        lax.all_gather(down_weight, "dp", axis=0, tiled=True),
        lax.all_gather(conv_two, "dp", axis=0, tiled=True),
    )
    my_index = lax.axis_index("space")
    slot_count = features.shape[1]
    chan_one = features.shape[2]
    chan_two = full_two.shape[0]
    half_xy = PXY // 2
    half_z = PZ // 2
    usable, source_dev, source_slot, living = slot_table(
        patch_home, patch_links, my_index, 0, slot_count
    )
    patch_field = features[0].reshape(slot_count, chan_one, PXY, PXY, PZ)
    padded = assemble(patch_field, patch_home, patch_links, my_index)
    stack_one = tap_stack(padded)
    pre_one = trim(conv_forward(stack_one, full_one, PXY), PXY, PZ)
    hidden_state = jax.nn.silu(pre_one).astype(jnp.bfloat16)
    reduced = down_forward(hidden_state, full_down).astype(jnp.bfloat16)
    padded_two = assemble(reduced, patch_home, patch_links, my_index)
    stack_two = tap_stack(padded_two)
    pre_two = trim(conv_forward(stack_two, full_two, half_xy), half_xy, half_z)
    live_cells = living[:, None, None, None, None]
    activated = jnp.where(live_cells, jax.nn.silu(pre_two), 0.0).astype(jnp.bfloat16)
    level_two = activated.reshape(1, slot_count, chan_two, half_xy * half_xy * half_z)
    grad_scale = float(lax.axis_size("dp") * patch_links.shape[0] * half_xy * half_xy * half_z) ** (
        -0.5
    )
    incoming = cotangent[0].reshape(pre_two.shape).astype(jnp.float32)
    grad_two = jnp.where(live_cells, incoming * silu_slope(pre_two) * grad_scale, 0.0).astype(
        jnp.bfloat16
    )
    ext_two = extend(grad_two)
    dw_two = weight_grad(stack_two, ext_two, half_xy)
    grad_padded = input_grad(ext_two, full_two, padded_two.shape)
    grad_reduced = disassemble(grad_padded, patch_home, patch_links, my_index).astype(jnp.bfloat16)
    dw_down, grad_hidden = down_backward(hidden_state, full_down, grad_reduced)
    grad_one = (grad_hidden * silu_slope(pre_one)).astype(jnp.bfloat16)
    dw_one = weight_grad(stack_one, extend(grad_one), PXY)
    owned = (
        lax.psum_scatter(dw_one.astype(jnp.bfloat16), "dp", scatter_dimension=0, tiled=True).astype(
            jnp.float32
        ),
        lax.psum_scatter(
            dw_down.astype(jnp.bfloat16), "dp", scatter_dimension=0, tiled=True
        ).astype(jnp.float32),
        lax.psum_scatter(dw_two.astype(jnp.bfloat16), "dp", scatter_dimension=0, tiled=True).astype(
            jnp.float32
        ),
    )
    shares = lax.psum((owned[0], owned[1], owned[2]), "space")
    return (level_two, shares[0], shares[1], shares[2])


def solution(mesh):
    in_specs = (
        P("dp", "space", None, None),
        P("dp", "space", None, None),
        P("dp", None),
        P("dp", None),
        P("dp", None),
        P(),
        P(),
    )
    out_specs = (P("dp", "space", None, None), P("dp", None), P("dp", None), P("dp", None))
    return jax.shard_map(
        on_device, mesh=mesh, in_specs=in_specs, out_specs=out_specs, check_vma=False
    )
```

profile of v0, /device:TPU:0, one launch (start us, length us, event | category | flops | bytes accessed | tf_op | source)
XLA Modules:
  0.0 357.1 jit_solution(11219825319108150353)
XLA Ops:
  17.9 3.0 collective-permute-start
  45.4 14.7 %all_gather.10 = bf16[128,512]{1,0:T(8,128)(2,1)S(1)} all-gather(bf16[32,512]{1,0:T(8,128)(2,1)S(1)} %copy-done.18), channel_id=1, replica_groups=mesh['dp'=4,'space'=8] {'dp'}, dimensions={0}, use_global_device_ids=true | all-gather | bytes 163840 | tf_op jit(solution)/shard_map/all_gather | solution.py:242
  60.9 20.8 %all_gather.11 = bf16[128,3456]{1,0:T(8,128)(2,1)S(1)} all-gather(bf16[32,3456]{1,0:T(8,128)(2,1)S(1)} %copy-done.13), channel_id=1, replica_groups=mesh['dp'=4,'space'=8] {'dp'}, dimensions={0}, use_global_device_ids=true | all-gather | bytes 1105920 | tf_op jit(solution)/shard_map/all_gather | solution.py:243
  81.7 14.2 %all_gather.9 = bf16[64,1728]{1,0:T(8,128)(2,1)S(1)} all-gather(bf16[16,1728]{1,0:T(8,128)(2,1)S(1)} %copy-done.17), channel_id=1, replica_groups=mesh['dp'=4,'space'=8] {'dp'}, dimensions={0}, use_global_device_ids=true | all-gather | bytes 276480 | tf_op jit(solution)/shard_map/all_gather | solution.py:241
  102.9 3.3 collective-permute-start.2
  112.6 6.1 %collective-permute-done.5 = bf16[3,2,64,72]{2,3,1,0:T(8,128)(2,1)S(1)} collective-permute-done((bf16[3,2,64,72]{2,3,1,0:T(8,128)(2,1)S(1)}, bf16[3,2,64,72]{2,3,1,0:T(8,128)(2,1)S(1)}, u32[]{:S(2)}, u32[]{:S(2)}) %collective-permute-start.5) | collective-permute-done | bytes 55328 | tf_op jit(solution)/shard_map/ppermute | solution.py:13
  118.9 3.2 select_maximum_fusion
  122.1 2.2 reshape.478
  133.2 2.6 fusion.24
  135.8 2.0 copy.514
  145.2 4.0 %collective-permute-done.7 = bf16[3,2,128,16]{2,0,3,1:T(4,128)(2,1)S(1)} collective-permute-done((bf16[3,2,128,16]{2,0,3,1:T(4,128)(2,1)S(1)}, bf16[3,2,128,16]{2,0,3,1:T(4,128)(2,1)S(1)}, u32[]{:S(2)}, u32[]{:S(2)}) %collective-permute-start.7) | collective-permute-done | bytes 24608 | tf_op jit(solution)/shard_map/ppermute | solution.py:13
  154.3 4.5 %collective-permute-start.9 = (bf16[3,2,128,20]{2,0,3,1:T(4,128)(2,1)S(1)}, bf16[3,2,128,20]{2,0,3,1:T(4,128)(2,1)S(1)}, u32[]{:S(2)}, u32[]{:S(2)}) collective-permute-start(bf16[3,2,128,20]{2,0,3,1:T(4,128)(2,1)S(1)} %copy_select_fusion.3), channel_id=1, source_target_pairs={{0,1},{1,2},{2,3},{3,4},{4,5},{5,6},{6,7},{8,9},{9,10},{10,11},{11... | collective-permute-start | bytes 92168 | tf_op jit(solution)/shard_map/ppermute | solution.py:13
  159.0 3.5 collective-permute-start.8
  165.6 4.5 %collective-permute-done.11 = bf16[3,2,128,20]{2,0,3,1:T(4,128)(2,1)S(1)} collective-permute-done((bf16[3,2,128,20]{2,0,3,1:T(4,128)(2,1)S(1)}, bf16[3,2,128,20]{2,0,3,1:T(4,128)(2,1)S(1)}, u32[]{:S(2)}, u32[]{:S(2)}) %collective-permute-start.11) | collective-permute-done | bytes 30752 | tf_op jit(solution)/shard_map/ppermute | solution.py:13
  186.2 7.4 %collective-permute-start.12 = (bf16[3,2,128,20]{2,0,3,1:T(4,128)(2,1)S(1)}, bf16[3,2,128,20]{2,0,3,1:T(4,128)(2,1)S(1)}, u32[]{:S(2)}, u32[]{:S(2)}) collective-permute-start(bf16[3,2,128,20]{2,0,3,1:T(4,128)(2,1)S(1)} %get-tuple-element.160), channel_id=1, source_target_pairs={{0,2},{1,3},{2,4},{3,5},{4,6},{5,7},{8,10},{9,11},{10,12},{11,13},... | collective-permute-start | bytes 92168 | tf_op jit(solution)/shard_map/ppermute | solution.py:13
  198.0 3.3 collective-permute-start.16
  202.1 2.2 fusion.75
  210.1 6.9 %fusion.80 = bf16[64,1,9,64]{3,0,2,1:T(8,128)(2,1)} fusion(bf16[3,9,64,18,96]{4,2,1,3,0:T(8,128)(2,1)} %copy-done.1, bf16[3,64,16,96]{3,1,2,0:T(8,128)(2,1)S(1)} %copy.591), kind=kOutput, calls=%fused_computation.93 | convolution fusion | flops 339775488 | bytes 7741440 | tf_op jit(solution)/shard_map/soxj,stcxj->otc/dot_general | solution.py:180
  217.0 6.9 %fusion.83 = bf16[64,1,9,64]{3,0,2,1:T(8,128)(2,1)} fusion(bf16[3,9,64,18,96]{4,2,1,3,0:T(8,128)(2,1)} %copy-done.1, bf16[3,64,16,96]{3,1,2,0:T(8,128)(2,1)S(1)} %copy.591), kind=kOutput, calls=%fused_computation.94 | convolution fusion | flops 339775488 | bytes 7741440 | tf_op jit(solution)/shard_map/soxj,stcxj->otc/dot_general | solution.py:180
  225.7 6.3 %fusion.77 = bf16[64,1,9,64]{3,0,2,1:T(8,128)(2,1)S(1)} fusion(bf16[3,9,64,18,96]{4,2,1,3,0:T(8,128)(2,1)} %copy-done.1, bf16[3,64,16,96]{3,1,2,0:T(8,128)(2,1)S(1)} %copy.591), kind=kOutput, calls=%fused_computation.92 | convolution fusion | flops 339775488 | bytes 7741440 | tf_op jit(solution)/shard_map/soxj,stcxj->otc/dot_general | solution.py:180
  237.7 12.4 %reduce-scatter.6.cloned.1.call-done = bf16[32,512]{1,0:T(8,128)(2,1)} async-done(((bf16[128,512]{1,0:T(8,128)(2,1)}), bf16[32,512]{1,0:T(8,128)(2,1)}) %reduce-scatter.6.cloned.1.call-update) | async-done | bytes 32784 | tf_op jit(solution)/shard_map/reduce_scatter | solution.py:284
  250.2 20.1 %reduce-scatter.10.cloned.1.call-done = bf16[16,1728]{1,0:T(8,128)(2,1)} async-done(((bf16[64,1728]{1,0:T(8,128)(2,1)}), bf16[16,1728]{1,0:T(8,128)(2,1)}) %reduce-scatter.10.cloned.1.call-update) | async-done | bytes 55312
  271.3 24.1 %reduce-scatter.8.cloned.1.call-done = bf16[32,3456]{1,0:T(8,128)(2,1)} async-done(((bf16[128,3456]{1,0:T(8,128)(2,1)}), bf16[32,3456]{1,0:T(8,128)(2,1)}) %reduce-scatter.8.cloned.1.call-update) | async-done | bytes 221200 | tf_op jit(solution)/shard_map/reduce_scatter | solution.py:287
  295.4 53.8 %all-reduce.35 = (f32[16,1728]{0,1:T(8,128)S(1)}, f32[32,512]{1,0:T(8,128)}, f32[32,3456]{1,0:T(8,128)}) all-reduce(bf16[16,1728]{0,1:T(8,128)(2,1)S(1)} %copy.644, bf16[32,512]{1,0:T(8,128)(2,1)} %reduce-scatter.6.cloned.1.call-done, bf16[32,3456]{1,0:T(8,128)(2,1)} %reduce-scatter.8.cloned.1.call-done), channel_id=1, replica_groups=mesh['dp'=4,'space'=8] {'space'}, use_global_device_ids=true, to_apply=%region_11.18 | all-reduce | flops 154624 | bytes 927744 | tf_op jit(solution)/shard_map/psum | solution.py:291
  (491 shorter events, 108.5 us)
Async XLA Ops:
  7.2 243.0 %reduce-scatter.6.cloned.1.call-start = ((), (), s32[]{:S(2)}) async-start(), calls=%async_computation.3 | async-start | bytes 163840 | tf_op jit(solution)/shard_map/reduce_scatter | solution.py:284
  15.7 84.5 %copy-start.26 = (pred[6]{0:T(512)(128)(4,1)}, pred[6]{0:T(512)(128)(4,1)S(1)}, u32[]{:S(2)}) copy-start(pred[6]{0:T(512)(128)(4,1)S(1)} %get-tuple-element.204) | copy-start | bytes 22
  16.1 82.3 %copy-start.4 = (bf16[1,3,64,1024]{2,3,1,0:T(8,128)(2,1)}, bf16[1,3,64,1024]{2,3,1,0:T(8,128)(2,1)S(1)}, u32[]{:S(2)}) copy-start(bf16[1,3,64,1024]{2,3,1,0:T(8,128)(2,1)S(1)} %copy.486) | copy-start | bytes 1179652
  17.9 79.3 %collective-permute-start = (bf16[3,2,64,64]{3,2,1,0:T(8,128)(2,1)}, bf16[3,2,64,64]{3,2,1,0:T(8,128)(2,1)}, u32[]{:S(2)}, u32[]{:S(2)}) collective-permute-start(bf16[3,2,64,64]{3,2,1,0:T(8,128)(2,1)} %broadcast_select_fusion.13), channel_id=1, source_target_pairs={{0,1},{1,2},{2,3},{3,4},{4,5},{5,6},{6,7},{8,9},{9,10},{10,11},{11... | collective-permute-start | bytes 147464 | tf_op jit(solution)/shard_map/ppermute | solution.py:13
  25.0 72.2 %collective-permute-start.1 = (bf16[3,2,64,64]{3,2,1,0:T(8,128)(2,1)}, bf16[3,2,64,64]{3,2,1,0:T(8,128)(2,1)}, u32[]{:S(2)}, u32[]{:S(2)}) collective-permute-start(bf16[3,2,64,64]{3,2,1,0:T(8,128)(2,1)} %broadcast_select_fusion.12), channel_id=1, source_target_pairs={{1,0},{2,1},{3,2},{4,3},{5,4},{6,5},{7,6},{9,8},{10,9},{11,10},{12... | collective-permute-start | bytes 147464 | tf_op jit(solution)/shard_map/ppermute | solution.py:13
  31.3 79.1 %copy-start.30 = (pred[6]{0:T(512)(128)(4,1)}, pred[6]{0:T(512)(128)(4,1)S(1)}, u32[]{:S(2)}) copy-start(pred[6]{0:T(512)(128)(4,1)S(1)} %get-tuple-element.205) | copy-start | bytes 22
  102.9 7.7 %collective-permute-start.2 = (bf16[3,2,64,72]{2,3,1,0:T(8,128)(2,1)S(1)}, bf16[3,2,64,72]{2,3,1,0:T(8,128)(2,1)S(1)}, u32[]{:S(2)}, u32[]{:S(2)}) collective-permute-start(bf16[3,2,64,72]{2,3,1,0:T(8,128)(2,1)S(1)} %broadcast_select_fusion.3), channel_id=1, source_target_pairs={{0,2},{1,3},{2,4},{3,5},{4,6},{5,7},{8,10},{9,11},{10,12},{11,13},... | collective-permute-start | bytes 165896 | tf_op jit(solution)/shard_map/ppermute | solution.py:13
  106.3 4.3 %collective-permute-start.3 = (bf16[3,2,64,72]{2,3,1,0:T(8,128)(2,1)S(1)}, bf16[3,2,64,72]{2,3,1,0:T(8,128)(2,1)S(1)}, u32[]{:S(2)}, u32[]{:S(2)}) collective-permute-start(bf16[3,2,64,72]{2,3,1,0:T(8,128)(2,1)S(1)} %broadcast_select_fusion.2), channel_id=1, source_target_pairs={{0,1},{1,2},{2,3},{3,4},{4,5},{5,6},{6,7},{8,9},{9,10},{10,11},{11... | collective-permute-start | bytes 165896 | tf_op jit(solution)/shard_map/ppermute | solution.py:13
  107.6 5.0 %collective-permute-start.4 = (bf16[3,2,64,72]{2,3,1,0:T(8,128)(2,1)S(1)}, bf16[3,2,64,72]{2,3,1,0:T(8,128)(2,1)S(1)}, u32[]{:S(2)}, u32[]{:S(2)}) collective-permute-start(bf16[3,2,64,72]{2,3,1,0:T(8,128)(2,1)S(1)} %broadcast_select_fusion.1), channel_id=1, source_target_pairs={{1,0},{2,1},{3,2},{4,3},{5,4},{6,5},{7,6},{9,8},{10,9},{11,10},{12... | collective-permute-start | bytes 165896 | tf_op jit(solution)/shard_map/ppermute | solution.py:13
  108.9 9.8 %collective-permute-start.5 = (bf16[3,2,64,72]{2,3,1,0:T(8,128)(2,1)S(1)}, bf16[3,2,64,72]{2,3,1,0:T(8,128)(2,1)S(1)}, u32[]{:S(2)}, u32[]{:S(2)}) collective-permute-start(bf16[3,2,64,72]{2,3,1,0:T(8,128)(2,1)S(1)} %broadcast_select_fusion), channel_id=1, source_target_pairs={{2,0},{3,1},{4,2},{5,3},{6,4},{7,5},{10,8},{11,9},{12,10},{13,11},... | collective-permute-start | bytes 165896 | tf_op jit(solution)/shard_map/ppermute | solution.py:13
  142.2 3.0 collective-permute-start.6
  143.9 5.4 %collective-permute-start.7 = (bf16[3,2,128,16]{2,0,3,1:T(4,128)(2,1)S(1)}, bf16[3,2,128,16]{2,0,3,1:T(4,128)(2,1)S(1)}, u32[]{:S(2)}, u32[]{:S(2)}) collective-permute-start(bf16[3,2,128,16]{2,0,3,1:T(4,128)(2,1)S(1)} %copy_select_fusion.5), channel_id=1, source_target_pairs={{1,0},{2,1},{3,2},{4,3},{5,4},{6,5},{7,6},{9,8},{10,9},{11,10},{12... | collective-permute-start | bytes 73736 | tf_op jit(solution)/shard_map/ppermute | solution.py:13
  154.3 11.2 %collective-permute-start.9 = (bf16[3,2,128,20]{2,0,3,1:T(4,128)(2,1)S(1)}, bf16[3,2,128,20]{2,0,3,1:T(4,128)(2,1)S(1)}, u32[]{:S(2)}, u32[]{:S(2)}) collective-permute-start(bf16[3,2,128,20]{2,0,3,1:T(4,128)(2,1)S(1)} %copy_select_fusion.3), channel_id=1, source_target_pairs={{0,1},{1,2},{2,3},{3,4},{4,5},{5,6},{6,7},{8,9},{9,10},{10,11},{11... | collective-permute-start | bytes 92168 | tf_op jit(solution)/shard_map/ppermute | solution.py:13
  159.0 6.6 %collective-permute-start.8 = (bf16[3,2,128,20]{2,0,3,1:T(4,128)(2,1)S(1)}, bf16[3,2,128,20]{2,0,3,1:T(4,128)(2,1)S(1)}, u32[]{:S(2)}, u32[]{:S(2)}) collective-permute-start(bf16[3,2,128,20]{2,0,3,1:T(4,128)(2,1)S(1)} %copy_select_fusion.4), channel_id=1, source_target_pairs={{0,2},{1,3},{2,4},{3,5},{4,6},{5,7},{8,10},{9,11},{10,12},{11,13},... | collective-permute-start | bytes 92168 | tf_op jit(solution)/shard_map/ppermute | solution.py:13
  162.5 3.1 collective-permute-start.10
  163.9 6.2 %collective-permute-start.11 = (bf16[3,2,128,20]{2,0,3,1:T(4,128)(2,1)S(1)}, bf16[3,2,128,20]{2,0,3,1:T(4,128)(2,1)S(1)}, u32[]{:S(2)}, u32[]{:S(2)}) collective-permute-start(bf16[3,2,128,20]{2,0,3,1:T(4,128)(2,1)S(1)} %copy_select_fusion), channel_id=1, source_target_pairs={{2,0},{3,1},{4,2},{5,3},{6,4},{7,5},{10,8},{11,9},{12,10},{13,11},... | collective-permute-start | bytes 92168 | tf_op jit(solution)/shard_map/ppermute | solution.py:13
  181.1 12.5 %collective-permute-start.13 = (bf16[3,2,128,20]{2,0,3,1:T(4,128)(2,1)S(1)}, bf16[3,2,128,20]{2,0,3,1:T(4,128)(2,1)S(1)}, u32[]{:S(2)}, u32[]{:S(2)}) collective-permute-start(bf16[3,2,128,20]{2,0,3,1:T(4,128)(2,1)S(1)} %get-tuple-element.158), channel_id=1, source_target_pairs={{0,1},{1,2},{2,3},{3,4},{4,5},{5,6},{6,7},{8,9},{9,10},{10,11},{11... | collective-permute-start | bytes 92168 | tf_op jit(solution)/shard_map/ppermute | solution.py:13
  183.6 12.0 %collective-permute-start.14 = (bf16[3,2,128,20]{2,0,3,1:T(4,128)(2,1)S(1)}, bf16[3,2,128,20]{2,0,3,1:T(4,128)(2,1)S(1)}, u32[]{:S(2)}, u32[]{:S(2)}) collective-permute-start(bf16[3,2,128,20]{2,0,3,1:T(4,128)(2,1)S(1)} %get-tuple-element.157), channel_id=1, source_target_pairs={{1,0},{2,1},{3,2},{4,3},{5,4},{6,5},{7,6},{9,8},{10,9},{11,10},{12... | collective-permute-start | bytes 92168 | tf_op jit(solution)/shard_map/ppermute | solution.py:13
  184.9 10.5 %collective-permute-start.15 = (bf16[3,2,128,20]{2,0,3,1:T(4,128)(2,1)S(1)}, bf16[3,2,128,20]{2,0,3,1:T(4,128)(2,1)S(1)}, u32[]{:S(2)}, u32[]{:S(2)}) collective-permute-start(bf16[3,2,128,20]{2,0,3,1:T(4,128)(2,1)S(1)} %get-tuple-element.159), channel_id=1, source_target_pairs={{2,0},{3,1},{4,2},{5,3},{6,4},{7,5},{10,8},{11,9},{12,10},{13,11},... | collective-permute-start | bytes 92168 | tf_op jit(solution)/shard_map/ppermute | solution.py:13
  186.2 9.0 %collective-permute-start.12 = (bf16[3,2,128,20]{2,0,3,1:T(4,128)(2,1)S(1)}, bf16[3,2,128,20]{2,0,3,1:T(4,128)(2,1)S(1)}, u32[]{:S(2)}, u32[]{:S(2)}) collective-permute-start(bf16[3,2,128,20]{2,0,3,1:T(4,128)(2,1)S(1)} %get-tuple-element.160), channel_id=1, source_target_pairs={{0,2},{1,3},{2,4},{3,5},{4,6},{5,7},{8,10},{9,11},{10,12},{11,13},... | collective-permute-start | bytes 92168 | tf_op jit(solution)/shard_map/ppermute | solution.py:13
  196.4 4.9 %collective-permute-start.17 = (bf16[3,2,128,16]{2,0,3,1:T(4,128)(2,1)S(1)}, bf16[3,2,128,16]{2,0,3,1:T(4,128)(2,1)S(1)}, u32[]{:S(2)}, u32[]{:S(2)}) collective-permute-start(bf16[3,2,128,16]{2,0,3,1:T(4,128)(2,1)S(1)} %get-tuple-element.164), channel_id=1, source_target_pairs={{1,0},{2,1},{3,2},{4,3},{5,4},{6,5},{7,6},{9,8},{10,9},{11,10},{12... | collective-permute-start | bytes 73736 | tf_op jit(solution)/shard_map/ppermute | solution.py:13
  198.0 3.9 %collective-permute-start.16 = (bf16[3,2,128,16]{2,0,3,1:T(4,128)(2,1)S(1)}, bf16[3,2,128,16]{2,0,3,1:T(4,128)(2,1)S(1)}, u32[]{:S(2)}, u32[]{:S(2)}) collective-permute-start(bf16[3,2,128,16]{2,0,3,1:T(4,128)(2,1)S(1)} %get-tuple-element.163), channel_id=1, source_target_pairs={{0,1},{1,2},{2,3},{3,4},{4,5},{5,6},{6,7},{8,9},{9,10},{10,11},{11... | collective-permute-start | bytes 73736 | tf_op jit(solution)/shard_map/ppermute | solution.py:13
  225.6 44.6 %reduce-scatter.10.cloned.1.call-start = ((), (), s32[]{:S(2)}) async-start(), calls=%async_computation.5 | async-start | bytes 286720
  233.3 62.1 %reduce-scatter.8.cloned.1.call-start = ((), (), s32[]{:S(2)}) async-start(), calls=%async_computation.4 | async-start | bytes 1105920 | tf_op jit(solution)/shard_map/reduce_scatter | solution.py:287
  (74 other events, 1512.2 us)
Sparse Core Ops, SparseCore 0:
  225.7 24.3 reduce-scatter.5
  252.5 17.6 reduce-scatter.9
  272.6 22.8 reduce-scatter.7
where the time goes:
time: 362 us; the launch traced here: 357 us
  blocking collectives  103 us (28%)
  waiting for transfers between devices  75.2 us (21%)
  local copies, waits for them, and re-layouts  65.7 us (18%)
  starting transfers between devices  41.9 us (12%)
  matrix products  36.9 us (10%)
  other arithmetic  17.2 us (5%)
  between operations  16.6 us (5%)
    psum x1, blocking collectives, on_device(): shares = lax.psum((owned[0], owned[1], owned[2]), 'space')  53.8 us
    ppermute x18, starting transfers between devices, shifted(): return lax.ppermute(value, axis, pairs)  41.8 us
    reduce_scatter x1, waiting for transfers between devices, on_device(): lax.psum_scatter(dw_two.astype(jnp.bfloat16), 'dp', scatter_dimension=0,...  24.1 us
    dot_general x6, matrix products, weight_grad(): jnp.einsum('soxj,stcxj->otc', grad_ext, stacked[:, :, :, shift_x:shift_x...  23.3 us
    all_gather x1, blocking collectives, on_device(): lax.all_gather(conv_two, 'dp', axis=0, tiled=True)  20.8 us
    unnamed x4, waiting for transfers between devices  20.1 us
    ppermute x18, waiting for transfers between devices, shifted(): return lax.ppermute(value, axis, pairs)  18.6 us
    all_gather x1, blocking collectives, on_device(): lax.all_gather(down_weight, 'dp', axis=0, tiled=True)  14.7 us
  transfers between devices with their start and end apart: 21, of which 10 were waited for; matrix products, arithmetic and copies ran while one was open for 11% of the time, Pallas kernels for 0%

commit v1 on v0

v1 whole, which is shorter than its diff:
```python
import functools

import jax
import jax.numpy as jnp
import numpy as np
from jax import lax
from jax.experimental import pallas as pl
from jax.experimental.pallas import tpu as pltpu
from jax.sharding import PartitionSpec as P

PXY = 16
PZ = 4
LEAD = 8
BF = jnp.bfloat16
F32 = jnp.float32
MESH = pl.DeviceIdType.MESH
VM = pl.BlockSpec(memory_space=pltpu.VMEM)
SM = pl.BlockSpec(memory_space=pltpu.SMEM)
BIG = 58 * 1024 * 1024


def up128(value):
    return -(-value // 128) * 128


def dot(a, b):
    return jnp.dot(a, b, preferred_element_type=F32)


def dot_nt(a, b):
    return lax.dot_general(a, b, (((1,), (1,)), ((), ())), preferred_element_type=F32)


def sigmoid(v):
    return 1.0 / (1.0 + jnp.exp(-v))


def onehot(rows, cols, pairs):
    m = np.zeros((rows, cols), np.float32)
    for r, c in pairs:
        m[r, c] = 1.0
    return jnp.asarray(m, BF)


class Level:
    def __init__(self, xy, z):
        self.xy, self.z = xy, z
        self.yz = xy * z
        self.cells = xy * xy * z
        self.stride = (xy + 2) * z
        self.out = up128(xy * self.stride)
        self.wide = up128(LEAD + self.out + 2 * self.stride + z + 1)

    def cell(self, x, y, k):
        return x * self.yz + y * self.z + k

    def pad(self, x, y, k):
        return LEAD + (x + 1) * self.stride + (y + 1) * self.z + k

    def pos(self, x, y, k):
        return x * self.stride + (y + 1) * self.z + k

    def shift(self, tap):
        dx, dy, dz = tap // 9 - 1, (tap // 3) % 3 - 1, tap % 3 - 1
        return LEAD + self.stride * (1 + dx) + self.z * dy + dz

    def all(self):
        r, q = range(self.xy), range(self.z)
        return [(x, y, k) for x in r for y in r for k in q]

    def face_y(self):
        last = self.xy - 1
        r, q = range(self.xy), range(self.z)
        pairs = []
        for x in r:
            for k in q:
                pairs.append((self.cell(x, 0, k), (x + 1) * self.z + k))
                pairs.append((self.cell(x, last, k), 128 + (x + 1) * self.z + k))
        return onehot(self.cells, 256, pairs)

    def rim_to_face_y(self):
        last = self.xy - 1
        pairs = []
        for k in range(self.z):
            for base, xe in ((0, self.xy + 1), (64, 0)):
                pairs.append((base + k, xe * self.z + k))
                pairs.append((base + last * self.z + k, 128 + xe * self.z + k))
        return onehot(128, 256, pairs)

    def place_x(self):
        pairs = []
        for y in range(self.xy):
            for k in range(self.z):
                pairs.append((y * self.z + k, self.pad(self.xy, y, k)))
                pairs.append((64 + y * self.z + k, self.pad(-1, y, k)))
        return onehot(128, self.wide, pairs)

    def place_y(self):
        pairs = []
        for xe in range(self.xy + 2):
            for k in range(self.z):
                pairs.append((xe * self.z + k, self.pad(xe - 1, self.xy, k)))
                pairs.append((128 + xe * self.z + k, self.pad(xe - 1, -1, k)))
        return onehot(256, self.wide, pairs)

    def place(self):
        return onehot(self.cells, self.wide, [(self.cell(*c), self.pad(*c)) for c in self.all()])


def barrier(lists):
    sem = pltpu.get_barrier_semaphore()
    for target in lists:
        pl.semaphore_signal(sem, inc=1, device_id=target, device_id_type=MESH)
    pl.semaphore_wait(sem, len(lists))


def near(n):
    me = lax.axis_index("space")
    return {k: lax.rem(me + k + n, n) for k in (-2, -1, 1, 2)}


def members(n, group):
    me = lax.axis_index("space")
    base = (me // group) * group
    mine = me - base
    return mine, [base + lax.rem(mine + k, group) for k in range(1, group)]


def swap(n, src, dst, reach, send, recv):
    ids = near(n)
    order = [k for k in range(-reach, reach + 1) if k != 0]
    copies = []
    for i, k in enumerate(order):
        copies.append(
            pltpu.make_async_remote_copy(
                src_ref=src,
                dst_ref=dst.at[i],
                send_sem=send.at[i],
                recv_sem=recv.at[i],
                device_id={"space": ids[-k]},
                device_id_type=MESH,
            )
        )
    for c in copies:
        c.start()
    return order, copies


def select(sel_ref, slots, own, got, order, upper, lower):
    width = own.shape[2]
    first = lax.broadcasted_iota(jnp.int32, (1, width), 1) < width // 2
    blocks = [(k, s, (own[s] if k == 0 else got[order.index(k), s]).astype(F32))
              for k in [0] + order for s in range(slots)]
    result = []
    for t in range(slots):
        total = None
        for k, s, block in blocks:
            at = lambda side: sel_ref[((side * slots + t) * 5 + k + 2) * slots + s]
            term = block * jnp.where(first, at(upper), at(lower))
            total = term if total is None else total + term
        result.append(total.astype(BF))
    return result


def halo_body(n, lv, slots, field, sel, e_face, e_rim, rx, ry, sx, sy, gx, gy, xs, xr, ys, yr):
    chan = field.shape[1]
    last = lv.cells - lv.yz
    sx[...] = jnp.zeros_like(sx)
    sx[:, :, 0 : lv.yz] = field[:, :, 0 : lv.yz]
    sx[:, :, 64 : 64 + lv.yz] = field[:, :, last : lv.cells]
    order, copies = swap(n, sx, gx, 1, xs, xr)
    base = dot(field[...].reshape(slots * chan, lv.cells), e_face[...])
    for c in copies:
        c.wait()
    rims = select(sel, slots, sx, gx, order, 1, 0)
    for s in range(slots):
        rx[s] = rims[s]
        sy[s] = (base[s * chan : (s + 1) * chan] + dot(rims[s], e_rim[...])).astype(BF)
    order, copies = swap(n, sy, gy, 2, ys, yr)
    for c in copies:
        c.wait()
    rims = select(sel, slots, sy, gy, order, 3, 2)
    for s in range(slots):
        ry[s] = rims[s]


def halo_scratch(slots, chan):
    return [
        pltpu.VMEM((slots, chan, 128), BF),
        pltpu.VMEM((slots, chan, 256), BF),
        pltpu.VMEM((2, slots, chan, 128), BF),
        pltpu.VMEM((4, slots, chan, 256), BF),
        pltpu.SemaphoreType.DMA((2,)),
        pltpu.SemaphoreType.DMA((2,)),
        pltpu.SemaphoreType.DMA((4,)),
        pltpu.SemaphoreType.DMA((4,)),
    ]


class Pack:
    def __init__(self, one, down, two, group):
        self.one, self.down, self.two = one, down, two
        self.rows = two[0]
        self.half = up128(-(-one[1] // 2))
        self.at_down = two[1]
        self.at_one = two[1] + down[1]
        self.total = -(-(self.at_one + self.half) // (group * 128)) * group * 128
        self.part = self.total // group
        self.rest = one[1] - self.half

    def put(self, dst, one, down, two):
        low = self.one[0]
        a = self.at_one
        dst[:, 0 : self.at_down] = two
        dst[:, self.at_down : a] = down
        dst[:, a:] = jnp.zeros((self.rows, self.total - a), dst.dtype)
        dst[0:low, a : a + self.half] = one[:, 0 : self.half]
        dst[low : 2 * low, a : a + self.rest] = one[:, self.half :]

    def lanes(self, index):
        return pl.ds(pl.multiple_of(index * self.part, 128), self.part)


def start_kernel(n, dps, group, lv, slots, pack, field, sel, e_face, e_rim, one, down, two, rx, ry, full,
                 packed, gath, zs, zr, ms, mr, *halo):
    dp = lax.axis_index("dp")
    mine, others = members(n, group)
    peers = [lax.rem(dp + k, dps) for k in range(1, dps)]
    pack.put(packed, one[...], down[...], two[...])
    barrier([{"space": t} for t in near(n).values()] + [{"space": t} for t in others]
            + [{"dp": t} for t in peers])
    lanes = pack.lanes(mine)
    zc = []
    for i, t in enumerate(peers):
        zc.append(pltpu.make_async_remote_copy(
            src_ref=packed.at[:, lanes], dst_ref=gath.at[dp, :, lanes],
            send_sem=zs.at[i], recv_sem=zr.at[i], device_id={"dp": t}, device_id_type=MESH))
    for c in zc:
        c.start()
    gath[dp] = packed[...]
    mc = []
    for i in range(dps - 1):
        zc[i].wait()
        source = lax.rem(dp + dps - 1 - i, dps)
        for j, t in enumerate(others):
            c = pltpu.make_async_remote_copy(
                src_ref=gath.at[source, :, lanes], dst_ref=gath.at[source, :, lanes],
                send_sem=ms.at[i, j], recv_sem=mr.at[i, j], device_id={"space": t}, device_id_type=MESH)
            c.start()
            mc.append((c, i, j))
    halo_body(n, lv, slots, field, sel, e_face, e_rim, rx, ry, *halo)
    for c, i, j in mc:
        c.wait()
    full[...] = gath[...]


def halo_kernel(n, lv, slots, field, sel, e_face, e_rim, rx, ry, *halo):
    barrier([{"space": t} for t in near(n).values()])
    halo_body(n, lv, slots, field, sel, e_face, e_rim, rx, ry, *halo)


def columns(lv, padded, chan, store):
    lane = lax.broadcasted_iota(jnp.int32, padded.shape, 1) % lv.z
    zero = jnp.zeros_like(padded)
    kinds = [jnp.where(lane == lv.z - 1, zero, padded), padded, jnp.where(lane == 0, zero, padded)]
    for tap in range(27):
        a = lv.shift(tap)
        store(tap, kinds[tap % 3][:, a : a + lv.out])


def unfold_one(pack, dps, full, w1):
    low = pack.one[0]
    a = pack.at_one
    for d in range(dps):
        w1[d * low : (d + 1) * low, 0 : pack.half] = full[d, 0:low, a : a + pack.half]
        w1[d * low : (d + 1) * low, pack.half :] = full[d, low : 2 * low, a : a + pack.rest]


def first_kernel(lv, slots, pack, dps, field, rx, ry, e_place, e_x, e_y, e_perm, full,
                 padded, pre, split, reduced, w1, xcol):
    chan = field.shape[1]
    unfold_one(pack, dps, full, w1)
    rows = slots * chan
    pad = (dot(field[...].reshape(rows, lv.cells), e_place[...])
           + dot(rx[...].reshape(rows, 128), e_x[...])
           + dot(ry[...].reshape(rows, 256), e_y[...])).astype(BF)
    down = full[:, :, pack.at_down : pack.at_one].reshape(dps * pack.rows, pack.down[1])
    cells = lv.cells // 8
    for s in range(slots):
        mine = pad[s * chan : (s + 1) * chan]
        padded[s] = mine

        def store(tap, value):
            xcol[tap * chan : (tap + 1) * chan] = value

        columns(lv, mine, chan, store)
        value = dot(w1[...], xcol[...])
        pre[s] = value
        hidden = (value * sigmoid(value)).astype(BF)
        parts = dot(hidden, e_perm[...]).astype(BF)
        stacked = jnp.concatenate([parts[:, e * cells : (e + 1) * cells] for e in range(8)], axis=0)
        split[s] = stacked
        reduced[s] = dot(down, stacked).astype(BF)


def second_kernel(lv, slots, pack, dps, scale, field, rx, ry, e_place, e_x, e_y, e_trim, e_spread, cot, live, full,
                  level, dw, gp, xcol, gcol, wt, gbuf):
    chan = field.shape[1]
    rows = slots * chan
    pad = (dot(field[...].reshape(rows, lv.cells), e_place[...])
           + dot(rx[...].reshape(rows, 128), e_x[...])
           + dot(ry[...].reshape(rows, 256), e_y[...])).astype(BF)
    w2 = full[:, :, 0 : pack.at_down].reshape(dps * pack.rows, pack.at_down)
    out = lv.out
    for s in range(slots):
        def store(tap, value):
            xcol[tap * chan : (tap + 1) * chan, s * out : (s + 1) * out] = value

        columns(lv, pad[s * chan : (s + 1) * chan], chan, store)
    pre = dot(w2, xcol[...])
    gbuf[...] = jnp.zeros_like(gbuf)
    lane = lax.broadcasted_iota(jnp.int32, (1, out), 1) % lv.z
    grads = []
    for s in range(slots):
        v = pre[:, s * out : (s + 1) * out]
        sg = sigmoid(v)
        act = dot((v * sg).astype(BF), e_trim[...])
        alive = live[s] > 0.5
        level[s] = jnp.where(alive, act, 0.0).astype(BF)
        inc = dot(cot[s], e_spread[...])
        g = jnp.where(alive, inc * (sg * (1.0 + v * (1.0 - sg))) * scale, 0.0)
        grads.append(g.astype(BF))
        for d in range(3):
            keep = lane >= 0 if d == 1 else (lane != 0 if d == 0 else lane != lv.z - 1)
            gbuf[d, :, 128 : 128 + out] = jnp.where(keep, g, 0.0).astype(BF)
        for tap in range(27):
            a = 128 - lv.shift(tap)
            gcol[tap * chan : (tap + 1) * chan, s * out : (s + 1) * out] = gbuf[tap % 3, :, a : a + out]
    for tap in range(27):
        wt[:, tap * chan : (tap + 1) * chan] = w2[:, tap * chan : (tap + 1) * chan].astype(F32).T.astype(BF)
    back = dot(wt[...], gcol[...])
    for s in range(slots):
        gp[s] = back[:, s * out : (s + 1) * out]
    dw[...] = dot_nt(jnp.concatenate(grads, axis=1), xcol[...]).astype(BF)


def back_kernel(n, lv, slots, gp, sel, e_gy, e_by, e_gx, e_dense, e_bx, out,
                sx, sy, gx, gy, xs, xr, ys, yr):
    barrier([{"space": t} for t in near(n).values()])
    for s in range(slots):
        sy[s] = dot(gp[s].astype(BF), e_gy[...]).astype(BF)
    order, copies = swap(n, sy, gy, 2, ys, yr)
    for c in copies:
        c.wait()
    back = select(sel, slots, sy, gy, order, 3, 2)
    dense = []
    for s in range(slots):
        w = gp[s] + dot(back[s], e_by[...])
        hi = w.astype(BF)
        low = (w - hi.astype(F32)).astype(BF)
        sx[s] = dot(hi, e_gx[...]).astype(BF)
        dense.append(dot(hi, e_dense[...]) + dot(low, e_dense[...]))
    order, copies = swap(n, sx, gx, 1, xs, xr)
    for c in copies:
        c.wait()
    back = select(sel, slots, sx, gx, order, 1, 0)
    for s in range(slots):
        out[s] = (dense[s] + dot(back[s], e_bx[...])).astype(BF)


def last_kernel(lv, slots, pack, dps, gr, split, pre, padded, e_up, kind, full, dw_one, dw_down, xcol):
    chan = pre.shape[1]
    down = full[:, :, pack.at_down : pack.at_one].reshape(dps * pack.rows, pack.down[1])
    down_t = down.astype(F32).T.astype(BF)
    total_down = None
    total_one = None
    for s in range(slots):
        g = gr[s]
        part = dot_nt(g, split[s])
        total_down = part if total_down is None else total_down + part
        up = dot(g, e_up[...]).astype(BF)
        eight = dot(down_t, up)
        gh = None
        for e in range(8):
            term = jnp.where(kind[...] == e, eight[e * chan : (e + 1) * chan], 0.0)
            gh = term if gh is None else gh + term
        v = pre[s]
        sg = sigmoid(v)
        g1 = (gh * (sg * (1.0 + v * (1.0 - sg)))).astype(BF)

        def store(tap, value):
            xcol[tap * chan : (tap + 1) * chan] = value

        columns(lv, padded[s], chan, store)
        part = dot_nt(g1, xcol[...])
        total_one = part if total_one is None else total_one + part
    dw_down[...] = total_down.astype(BF)
    dw_one[...] = total_one.astype(BF)


def reduce_kernel(n, dps, group, pack, one, down, two, o_one, o_down, o_two,
                  packed, rs, acc, zb, fin, ms, mr, zs, zr, fs, fr):
    dp = lax.axis_index("dp")
    mine, others = members(n, group)
    me = lax.axis_index("space")
    base = me - mine
    peers = [lax.rem(dp + k, dps) for k in range(1, dps)]
    r1, r2 = pack.one[0], pack.rows
    for d in range(dps):
        pack.put(packed.at[d], one[d * r1 : (d + 1) * r1], down[d * r2 : (d + 1) * r2], two[d * r2 : (d + 1) * r2])
    barrier([{"space": t} for t in others] + [{"dp": t} for t in peers])
    lanes = pack.lanes(mine)
    copies = []
    for j, t in enumerate(others):
        c = pltpu.make_async_remote_copy(
            src_ref=packed.at[:, :, pack.lanes(t - base)], dst_ref=rs.at[j],
            send_sem=ms.at[j], recv_sem=mr.at[j], device_id={"space": t}, device_id_type=MESH)
        c.start()
        copies.append(c)
    total = packed[:, :, lanes].astype(F32)
    for j, c in enumerate(copies):
        c.wait()
        total = total + rs[j].astype(F32)
    acc[...] = total.astype(BF)
    copies = []
    for j, t in enumerate(peers):
        c = pltpu.make_async_remote_copy(
            src_ref=acc.at[t], dst_ref=zb.at[j],
            send_sem=zs.at[j], recv_sem=zr.at[j], device_id={"dp": t}, device_id_type=MESH)
        c.start()
        copies.append(c)
    total = acc[dp].astype(F32)
    for j, c in enumerate(copies):
        c.wait()
        total = total + zb[j].astype(F32)
    fin[:, lanes] = total.astype(BF)
    copies = []
    for j, t in enumerate(others):
        c = pltpu.make_async_remote_copy(
            src_ref=fin.at[:, lanes], dst_ref=fin.at[:, lanes],
            send_sem=fs.at[j], recv_sem=fr.at[j], device_id={"space": t}, device_id_type=MESH)
        c.start()
        copies.append(c)
    for c in copies:
        c.wait()
    a = pack.at_one
    o_two[...] = fin[:, 0 : pack.at_down].astype(F32)
    o_down[...] = fin[:, pack.at_down : a].astype(F32)
    o_one[:, 0 : pack.half] = fin[0:r1, a : a + pack.half].astype(F32)
    o_one[:, pack.half :] = fin[r1 : 2 * r1, a : a + pack.rest].astype(F32)


def call(body, args, specs, outs, scratch, ident=None):
    extra = {} if ident is None else {"collective_id": ident, "has_side_effects": True}
    return pl.pallas_call(
        body,
        out_shape=[jax.ShapeDtypeStruct(s, t) for s, t in outs],
        in_specs=specs,
        out_specs=[VM] * len(outs),
        scratch_shapes=scratch,
        compiler_params=pltpu.CompilerParams(vmem_limit_bytes=BIG, **extra),
    )(*args)


def on_device(features, cotangent, conv_one, down_weight, conv_two, patch_home, patch_links):
    n, dps = lax.axis_size("space"), lax.axis_size("dp")
    group = 8 if n % 8 == 0 else n
    slots, c1 = features.shape[1], features.shape[2]
    c2 = conv_two.shape[0] * dps
    me = lax.axis_index("space")
    one, two = Level(PXY, PZ), Level(PXY // 2, PZ // 2)
    pack = Pack(conv_one.shape, down_weight.shape, conv_two.shape, group)

    own = patch_home[None, :] == (me * slots + jnp.arange(slots, dtype=jnp.int32))[:, None]
    live = jnp.any(own, axis=1).astype(F32)
    ids = jnp.arange(patch_home.shape[0], dtype=jnp.int32)
    codes = (me - 2) * slots + jnp.arange(5 * slots, dtype=jnp.int32)
    target = jnp.max(jnp.where(own[:, :, None], patch_links[None], -1), axis=1)
    source = jnp.max(jnp.where(target[:, :, None] == ids, patch_home, -1), axis=2)
    sel = ((source.T[:, :, None] == codes) & (source.T[:, :, None] >= 0)).astype(F32).reshape(-1)

    field = features[0]
    dma = pltpu.SemaphoreType.DMA
    rx, ry, full = call(
        functools.partial(start_kernel, n, dps, group, one, slots, pack),
        (field, sel, one.face_y(), one.rim_to_face_y(), conv_one, down_weight, conv_two),
        [VM, SM, VM, VM, VM, VM, VM],
        [((slots, c1, 128), BF), ((slots, c1, 256), BF), ((dps, pack.rows, pack.total), BF)],
        [pltpu.VMEM((pack.rows, pack.total), BF), pltpu.VMEM((dps, pack.rows, pack.total), BF),
         dma((dps - 1,)), dma((dps - 1,)), dma((dps - 1, group - 1)), dma((dps - 1, group - 1))]
        + halo_scratch(slots, c1),
        0,
    )

    cells_two = two.cells
    perm = []
    spot = []
    kind = np.full((1, one.out), -1, np.int32)
    for x, y, k in one.all():
        e = (x % 2) * 4 + (y % 2) * 2 + k % 2
        small = two.cell(x // 2, y // 2, k // 2)
        at = one.pos(x, y, k)
        perm.append((at, e * cells_two + small))
        spot.append((small, at))
        kind[0, at] = e
    padded, pre, split, reduced = call(
        functools.partial(first_kernel, one, slots, pack, dps),
        (field, rx, ry, one.place(), one.place_x(), one.place_y(), onehot(one.out, one.cells, perm), full),
        [VM] * 8,
        [((slots, c1, one.wide), BF), ((slots, c1, one.out), F32), ((slots, 8 * c1, cells_two), BF),
         ((slots, c2, cells_two), BF)],
        [pltpu.VMEM((c1, conv_one.shape[1]), BF), pltpu.VMEM((27 * c1, one.out), BF)],
    )

    rx2, ry2 = call(
        functools.partial(halo_kernel, n, two, slots),
        (reduced, sel, two.face_y(), two.rim_to_face_y()),
        [VM, SM, VM, VM],
        [((slots, c2, 128), BF), ((slots, c2, 256), BF)],
        halo_scratch(slots, c2),
        1,
    )

    scale = float(dps * patch_links.shape[0] * cells_two) ** (-0.5)
    trim = [(two.pos(*c), two.cell(*c)) for c in two.all()]
    level, dw_two, gp = call(
        functools.partial(second_kernel, two, slots, pack, dps, scale),
        (reduced, rx2, ry2, two.place(), two.place_x(), two.place_y(), onehot(two.out, cells_two, trim),
         onehot(cells_two, two.out, [(b, a) for a, b in trim]), cotangent[0], live, full),
        [VM] * 9 + [SM, VM],
        [((slots, c2, cells_two), BF), ((c2, 27 * c2), BF), ((slots, c2, two.out), F32)],
        [pltpu.VMEM((27 * c2, slots * two.out), BF), pltpu.VMEM((27 * c2, slots * two.out), BF),
         pltpu.VMEM((c2, 27 * c2), BF), pltpu.VMEM((3, c2, 256 + two.out), BF)],
    )

    last = two.xy - 1
    g_y, b_y, g_x, b_x = [], [], [], []
    for k in range(two.z):
        for xe in range(two.xy + 2):
            lane = xe * two.z + k
            g_y += [(two.pad(xe - 1, -1, k), lane), (two.pad(xe - 1, two.xy, k), 128 + lane)]
            b_y += [(lane, two.pad(xe - 1, last, k)), (128 + lane, two.pad(xe - 1, 0, k))]
        for y in range(two.xy):
            lane = y * two.z + k
            g_x += [(two.pad(-1, y, k), lane), (two.pad(two.xy, y, k), 64 + lane)]
            b_x += [(lane, two.cell(last, y, k)), (64 + lane, two.cell(0, y, k))]
    dense = [(two.pad(*c), two.cell(*c)) for c in two.all()]
    [gr] = call(
        functools.partial(back_kernel, n, two, slots),
        (gp, sel, onehot(two.out, 256, g_y), onehot(256, two.out, b_y), onehot(two.out, 128, g_x),
         onehot(two.out, cells_two, dense), onehot(128, cells_two, b_x)),
        [VM, SM, VM, VM, VM, VM, VM],
        [((slots, c2, cells_two), BF)],
        halo_scratch(slots, c2),
        2,
    )

    dw_one, dw_down = call(
        functools.partial(last_kernel, one, slots, pack, dps),
        (gr, split, pre, padded, onehot(cells_two, one.out, spot), jnp.asarray(kind), full),
        [VM] * 7,
        [((c1, 27 * c1), BF), ((c2, 8 * c1), BF)],
        [pltpu.VMEM((27 * c1, one.out), BF)],
    )

    outs = call(
        functools.partial(reduce_kernel, n, dps, group, pack),
        (dw_one, dw_down, dw_two),
        [VM] * 3,
        [(conv_one.shape, F32), (down_weight.shape, F32), (conv_two.shape, F32)],
        [pltpu.VMEM((dps, pack.rows, pack.total), BF), pltpu.VMEM((group - 1, dps, pack.rows, pack.part), BF),
         pltpu.VMEM((dps, pack.rows, pack.part), BF), pltpu.VMEM((dps - 1, pack.rows, pack.part), BF),
         pltpu.VMEM((pack.rows, pack.total), BF),
         dma((group - 1,)), dma((group - 1,)), dma((dps - 1,)), dma((dps - 1,)), dma((group - 1,)), dma((group - 1,))],
        3,
    )
    if n > group:
        rings = [[a + m for a in range(0, n, group)] for m in range(group)]
        outs = [lax.psum(o, "space", axis_index_groups=rings) for o in outs]
    return (level[None], outs[0], outs[1], outs[2])


def solution(mesh):
    weights = P("dp", None)
    slabs = P("dp", "space", None, None)
    return jax.shard_map(
        on_device,
        mesh=mesh,
        in_specs=(slabs, slabs, weights, weights, weights, P(), P()),
        out_specs=(slabs, weights, weights, weights),
        check_vma=False,
    )
```

time: 362 us -> 146 us (0.40); the launches traced: 357 us -> 146 us
  Pallas kernels: 0 us -> 136 us
  blocking collectives: 103 us -> 0 us
  waiting for transfers between devices: 75.2 us -> 0 us
  local copies, waits for them, and re-layouts: 65.7 us -> 5.69 us
  starting transfers between devices: 41.9 us -> 0 us
  matrix products: 36.9 us -> 0 us
  between operations: 16.6 us -> 0.7 us
  other arithmetic: 17.2 us -> 3.16 us
    pallas_call x0 -> x7, Pallas kernels: none -> 136 us  [call(): pl.pallas_call(body, out_shape=[jax.ShapeDtypeStruct(s, t) for s, t in ou...]
    psum x1 -> x0, blocking collectives: 53.8 us -> none  [on_device(): shares = lax.psum((owned[0], owned[1], owned[2]), 'space')]
    all_gather x3 -> x0, blocking collectives: 49.7 us -> none  [the longest x1 20.8 us: on_device(): lax.all_gather(conv_two, 'dp', axis=0, tiled=True)]
    ppermute x18 -> x0, starting transfers between devices: 41.8 us -> none  [shifted(): return lax.ppermute(value, axis, pairs)]
    dot_general x26 -> x0, matrix products: 36.9 us -> none  [the longest x6 23.3 us: weight_grad(): jnp.einsum('soxj,stcxj->otc', grad_ext, stacked[:, :, :, shift_x:shift_x...]
    reduce_scatter x2 -> x0, waiting for transfers between devices: 36.5 us -> none  [the longest x1 24.1 us: on_device(): lax.psum_scatter(dw_two.astype(jnp.bfloat16), 'dp', scatter_dimension=0,...]
    unnamed x4 -> x0, waiting for transfers between devices: 20.1 us -> none
    gather x37 -> x0, local copies, waits for them, and re-layouts: 19.2 us -> none  [the longest x16 9.88 us: outgoing(): jnp.take(flipped, take_at.reshape(-1), axis=0).reshape(face_set.shape)]
  transfers between devices with their start and end apart: 21 -> 0, of which waited for: 10 -> 0; matrix products, arithmetic and copies ran while one was open for 11% -> 0% of each run, Pallas kernels for 0% -> 0%
where the time goes in v1:
time: 146 us
  Pallas kernels  136 us (93%)
  local copies, waits for them, and re-layouts  5.69 us (4%)
  other arithmetic  3.16 us (2%)
    pallas_call x7, Pallas kernels, call(): pl.pallas_call(body, out_shape=[jax.ShapeDtypeStruct(s, t) for s, t in ou...  136 us
    unnamed x3, local copies, waits for them, and re-layouts  4.83 us

profile of v1, /device:TPU:0, one launch (start us, length us, event | category | flops | bytes accessed | tf_op | source)
XLA Modules:
  0.0 145.6 jit_solution(13671421886765194654)
XLA Ops:
  0.7 0.8 fusion
  1.5 0.5 convert_element_type.12.live
  2.0 0.8 select_reduce_fusion.1
  2.9 0.9 select_reduce_fusion
  3.7 0.1 copy.36
  3.9 0.1 copy.35
  3.9 0.1 and_convert_fusion
  4.0 0.7 reshape.55.sel
  4.7 32.0 %shard_map.282 = (bf16[3,64,128]{2,1,0:T(8,128)(2,1)}, bf16[3,64,256]{2,1,0:T(8,128)(2,1)}, bf16[4,32,5120]{2,1,0:T(8,128)(2,1)}) custom-call(bf16[3,64,1024]{2,1,0:T(8,128)(2,1)} %bitcast.5, f32[180]{0:T(256)} %reshape.55.sel, bf16[1024,256]{1,0:T(8,128)(2,1)} %constant.57.clone.e_face, bf16[128,256]{1,0:T(8,128)(2,1)} %constant.58.clone.e_rim, ...), custom_call_target="tpu_custom_call" | custom-call | tf_op jit(solution)/shard_map/pallas_call | solution.py:455
  36.7 9.7 %shard_map.283 = (bf16[3,64,1408]{2,1,0:T(8,128)(2,1)}, f32[3,64,1152]{2,1,0:T(8,128)}, bf16[3,512,128]{2,1,0:T(8,128)(2,1)}, bf16[3,128,128]{2,1,0:T(8,128)(2,1)}) custom-call(bf16[3,64,1024]{2,1,0:T(8,128)(2,1)} %bitcast.6, bf16[3,64,128]{2,1,0:T(8,128)(2,1)} %get-tuple-element.21.rx, bf16[3,64,256]{2,1,0:T(8,128)(2,1)} %get-tuple-element.22.ry, ...), custom_call_target="tpu_custom_call" | custom-call | tf_op jit(solution)/shard_map/pallas_call | solution.py:455
  46.4 23.3 %shard_map.284 = (bf16[3,128,128]{2,1,0:T(8,128)(2,1)}, bf16[3,128,256]{2,1,0:T(8,128)(2,1)}) custom-call(bf16[3,128,128]{2,1,0:T(8,128)(2,1)} %get-tuple-element.24.field, f32[180]{0:T(256)} %reshape.55.sel, bf16[128,256]{1,0:T(8,128)(2,1)} %constant.63.clone.e_face, bf16[128,256]{1,0:T(8,128)(2,1)} %constant.64.clone.e_rim), custom_call_target="tpu_custom_call" | custom-call | tf_op jit(solution)/shard_map/pallas_call | solution.py:455
  69.7 11.0 %shard_map.285 = (bf16[3,128,128]{2,1,0:T(8,128)(2,1)}, bf16[128,3456]{1,0:T(8,128)(2,1)}, f32[3,128,256]{2,1,0:T(8,128)}) custom-call(bf16[3,128,128]{2,1,0:T(8,128)(2,1)} %get-tuple-element.24.field, bf16[3,128,128]{2,1,0:T(8,128)(2,1)} %get-tuple-element.25.rx, bf16[3,128,256]{2,1,0:T(8,128)(2,1)} %get-tuple-element.26.ry, ...), custom_call_target="tpu_custom_call" | custom-call | tf_op jit(solution)/shard_map/pallas_call | solution.py:455
  80.7 22.0 %shard_map.286.gr = bf16[3,128,128]{2,1,0:T(8,128)(2,1)} custom-call(f32[3,128,256]{2,1,0:T(8,128)} %get-tuple-element.28.gp, f32[180]{0:T(256)} %reshape.55.sel, bf16[256,256]{1,0:T(8,128)(2,1)} %constant.70.clone.e_gy, bf16[256,256]{1,0:T(8,128)(2,1)} %constant.71.clone.e_by, bf16[256,128]{1,0:T(8,128)(2,1)} %constant.72.clone.e_gx, ...), custom_call_target="tpu_custom_call" | custom-call | tf_op jit(solution)/shard_map/pallas_call | solution.py:455
  102.7 8.5 %shard_map.287 = (bf16[64,1728]{1,0:T(8,128)(2,1)}, bf16[128,512]{1,0:T(8,128)(2,1)}) custom-call(bf16[3,128,128]{2,1,0:T(8,128)(2,1)} %shard_map.286.gr, bf16[3,512,128]{2,1,0:T(8,128)(2,1)} %get-tuple-element.29.split, f32[3,64,1152]{2,1,0:T(8,128)} %get-tuple-element.30.pre, bf16[3,64,1408]{2,1,0:T(8,128)(2,1)} %get-tuple-element.31.padded, ...), custom_call_target="tpu_custom_call" | custom-call | tf_op jit(solution)/shard_map/pallas_call | solution.py:455
  111.2 29.6 %shard_map.288 = (f32[16,1728]{1,0:T(8,128)}, f32[32,512]{1,0:T(8,128)}, f32[32,3456]{1,0:T(8,128)}) custom-call(bf16[64,1728]{1,0:T(8,128)(2,1)} %get-tuple-element.32.one, bf16[128,512]{1,0:T(8,128)(2,1)} %get-tuple-element.33.down, bf16[128,3456]{1,0:T(8,128)(2,1)} %get-tuple-element.34.two), custom_call_target="tpu_custom_call" | custom-call | tf_op jit(solution)/shard_map/pallas_call | solution.py:455
  140.8 1.6 %copy.40 = f32[16,1728]{1,0:T(8,128)} copy(f32[16,1728]{1,0:T(8,128)} %get-tuple-element.45) | data formatting | bytes 221184
  142.4 1.5 %copy.41 = f32[32,512]{1,0:T(8,128)} copy(f32[32,512]{1,0:T(8,128)} %get-tuple-element.46) | data formatting | bytes 131072
  143.8 1.8 %copy.42 = f32[32,3456]{1,0:T(8,128)} copy(f32[32,3456]{1,0:T(8,128)} %get-tuple-element.47) | data formatting | bytes 884736
  (3 shorter events, 0.0 us)

commit v2 on v1

--- a/solution.py
+++ b/solution.py
@@ -121,9 +121,12 @@
 
 def members(n, group):
     me = lax.axis_index("space")
-    base = (me // group) * group
-    mine = me - base
-    return mine, [base + lax.rem(mine + k, group) for k in range(1, group)]
+    inside = lax.rem(me, group)
+    base = me - inside
+    core, chip = lax.rem(inside, 2), inside // 2
+    chips = group // 2
+    others = [lax.rem(chip + k, chips) for k in range(1, chips)]
+    return core, chip, base + 2 * chip + 1 - core, others, [base + 2 * t + core for t in others]
 
 
 def swap(n, src, dst, reach, send, recv):
@@ -162,7 +165,7 @@
     return result
 
 
-def halo_body(n, lv, slots, field, sel, e_face, e_rim, rx, ry, sx, sy, gx, gy, xs, xr, ys, yr):
+def halo_body(n, lv, slots, field, sel, e_face, e_rim, rx, ry, sx, sy, gx, gy, xs, xr, ys, yr, between):
     chan = field.shape[1]
     last = lv.cells - lv.yz
     sx[...] = jnp.zeros_like(sx)
@@ -177,6 +180,7 @@
         rx[s] = rims[s]
         sy[s] = (base[s * chan : (s + 1) * chan] + dot(rims[s], e_rim[...])).astype(BF)
     order, copies = swap(n, sy, gy, 2, ys, yr)
+    between()
     for c in copies:
         c.wait()
     rims = select(sel, slots, sy, gy, order, 3, 2)
@@ -221,42 +225,92 @@
         return pl.ds(pl.multiple_of(index * self.part, 128), self.part)
 
 
+def remote(src, dst, send, recv, target):
+    return pltpu.make_async_remote_copy(
+        src_ref=src, dst_ref=dst, send_sem=send, recv_sem=recv, device_id=target, device_id_type=MESH
+    )
+
+
 def start_kernel(n, dps, group, lv, slots, pack, field, sel, e_face, e_rim, one, down, two, rx, ry, full,
-                 packed, gath, zs, zr, ms, mr, *halo):
+                 packed, gath, zs, zr, ms, mr, ps, pr, *halo):
     dp = lax.axis_index("dp")
-    mine, others = members(n, group)
+    core, chip, sibling, others, targets = members(n, group)
+    chips = group // 2
     peers = [lax.rem(dp + k, dps) for k in range(1, dps)]
     pack.put(packed, one[...], down[...], two[...])
-    barrier([{"space": t} for t in near(n).values()] + [{"space": t} for t in others]
+    barrier([{"space": t} for t in near(n).values()] + [{"space": t} for t in targets + [sibling]]
             + [{"dp": t} for t in peers])
-    lanes = pack.lanes(mine)
+    lanes = pack.lanes(core * chips + chip)
     zc = []
     for i, t in enumerate(peers):
-        zc.append(pltpu.make_async_remote_copy(
-            src_ref=packed.at[:, lanes], dst_ref=gath.at[dp, :, lanes],
-            send_sem=zs.at[i], recv_sem=zr.at[i], device_id={"dp": t}, device_id_type=MESH))
+        zc.append(remote(packed.at[:, lanes], gath.at[dp, :, lanes], zs.at[i], zr.at[i], {"dp": t}))
     for c in zc:
         c.start()
     gath[dp] = packed[...]
-    mc = []
+    mc, sc = [], []
+    shares = [lax.rem(dp + dps - 1 - i, dps) for i in range(dps - 1)]
     for i in range(dps - 1):
         zc[i].wait()
-        source = lax.rem(dp + dps - 1 - i, dps)
-        for j, t in enumerate(others):
-            c = pltpu.make_async_remote_copy(
-                src_ref=gath.at[source, :, lanes], dst_ref=gath.at[source, :, lanes],
-                send_sem=ms.at[i, j], recv_sem=mr.at[i, j], device_id={"space": t}, device_id_type=MESH)
+        block = gath.at[shares[i], :, lanes]
+        for j, t in enumerate(targets):
+            c = remote(block, block, ms.at[i, j], mr.at[i, j], {"space": t})
             c.start()
-            mc.append((c, i, j))
-    halo_body(n, lv, slots, field, sel, e_face, e_rim, rx, ry, *halo)
-    for c, i, j in mc:
+            mc.append(c)
+        c = remote(block, block, ps.at[i, chips - 1], pr.at[i, chips - 1], {"space": sibling})
+        c.start()
+        sc.append(c)
+
+    def between():
+        for i in range(dps - 1):
+            for j in range(chips - 1):
+                mc[i * (chips - 1) + j].wait()
+                sender = lax.rem(chip + chips - 1 - j, chips)
+                block = gath.at[shares[i], :, pack.lanes(core * chips + sender)]
+                c = remote(block, block, ps.at[i, j], pr.at[i, j], {"space": sibling})
+                c.start()
+                sc.append(c)
+
+    halo_body(n, lv, slots, field, sel, e_face, e_rim, rx, ry, *halo, between)
+    for c in sc:
         c.wait()
     full[...] = gath[...]
 
 
-def halo_kernel(n, lv, slots, field, sel, e_face, e_rim, rx, ry, *halo):
+def routed(block, got, order, route):
+    total = dot(block[...], route[2])
+    for i, k in enumerate(order):
+        total = total + dot(got[i], route[k + 2])
+    return total.astype(BF)
+
+
+def halo_kernel(n, lv, slots, field, way_x, way_y, e_x, e_y, e_rim, rx, ry, sx, sy, gx, gy, xs, xr, ys, yr):
+    wide = jnp.concatenate([field[s] for s in range(slots)], axis=1)
+    sx[...] = dot(wide, e_x[...]).astype(BF)
     barrier([{"space": t} for t in near(n).values()])
-    halo_body(n, lv, slots, field, sel, e_face, e_rim, rx, ry, *halo)
+    order, copies = swap(n, sx, gx, 1, xs, xr)
+    base = dot(wide, e_y[...])
+    for c in copies:
+        c.wait()
+    rim = routed(sx, gx, order, way_x)
+    rx[...] = rim
+    sy[...] = (base + dot(rim, e_rim[...])).astype(BF)
+    order, copies = swap(n, sy, gy, 2, ys, yr)
+    for c in copies:
+        c.wait()
+    ry[...] = routed(sy, gy, order, way_y)
+
+
+def packed_scratch(chan):
+    return [
+        pltpu.VMEM((chan, 128), BF),
+        pltpu.VMEM((chan, 128), BF),
+        pltpu.VMEM((2, chan, 128), BF),
+        pltpu.VMEM((4, chan, 128), BF),
+        pltpu.SemaphoreType.DMA((2,)),
+        pltpu.SemaphoreType.DMA((2,)),
+        pltpu.SemaphoreType.DMA((4,)),
+        pltpu.SemaphoreType.DMA((4,)),
+    ]
 
 
 def columns(lv, padded, chan, store):
@@ -306,17 +360,14 @@
 def second_kernel(lv, slots, pack, dps, scale, field, rx, ry, e_place, e_x, e_y, e_trim, e_spread, cot, live, full,
                   level, dw, gp, xcol, gcol, wt, gbuf):
     chan = field.shape[1]
-    rows = slots * chan
-    pad = (dot(field[...].reshape(rows, lv.cells), e_place[...])
-           + dot(rx[...].reshape(rows, 128), e_x[...])
-           + dot(ry[...].reshape(rows, 256), e_y[...])).astype(BF)
     w2 = full[:, :, 0 : pack.at_down].reshape(dps * pack.rows, pack.at_down)
     out = lv.out
     for s in range(slots):
         def store(tap, value):
             xcol[tap * chan : (tap + 1) * chan, s * out : (s + 1) * out] = value
 
-        columns(lv, pad[s * chan : (s + 1) * chan], chan, store)
+        pad = dot(field[s], e_place[...]) + dot(rx[...], e_x[s]) + dot(ry[...], e_y[s])
+        columns(lv, pad.astype(BF), chan, store)
     pre = dot(w2, xcol[...])
     gbuf[...] = jnp.zeros_like(gbuf)
     lane = lax.broadcasted_iota(jnp.int32, (1, out), 1) % lv.z
@@ -344,28 +395,35 @@
     dw[...] = dot_nt(jnp.concatenate(grads, axis=1), xcol[...]).astype(BF)
 
 
-def back_kernel(n, lv, slots, gp, sel, e_gy, e_by, e_gx, e_dense, e_bx, out,
+def back_kernel(n, slots, gp, way_x, way_y, e_gy, e_by, e_gx, e_dense, e_bx, out,
                 sx, sy, gx, gy, xs, xr, ys, yr):
+    total = None
+    for s in range(slots):
+        part = dot(gp[s].astype(BF), e_gy[s])
+        total = part if total is None else total + part
+    sy[...] = total.astype(BF)
     barrier([{"space": t} for t in near(n).values()])
-    for s in range(slots):
-        sy[s] = dot(gp[s].astype(BF), e_gy[...]).astype(BF)
     order, copies = swap(n, sy, gy, 2, ys, yr)
     for c in copies:
         c.wait()
-    back = select(sel, slots, sy, gy, order, 3, 2)
+    back = routed(sy, gy, order, way_y)
     dense = []
-    for s in range(slots):
-        w = gp[s] + dot(back[s], e_by[...])
+    total = None
+    for s in range(slots):
+        w = gp[s] + dot(back, e_by[s])
         hi = w.astype(BF)
         low = (w - hi.astype(F32)).astype(BF)
-        sx[s] = dot(hi, e_gx[...]).astype(BF)
-        dense.append(dot(hi, e_dense[...]) + dot(low, e_dense[...]))
+        part = dot(hi, e_gx[s])
+        total = part if total is None else total + part
+        dense.append((hi, low))
+    sx[...] = total.astype(BF)
     order, copies = swap(n, sx, gx, 1, xs, xr)
+    dense = [dot(hi, e_dense[...]) + dot(low, e_dense[...]) for hi, low in dense]
     for c in copies:
         c.wait()
-    back = select(sel, slots, sx, gx, order, 1, 0)
-    for s in range(slots):
-        out[s] = (dense[s] + dot(back[s], e_bx[...])).astype(BF)
+    back = routed(sx, gx, order, way_x)
+    for s in range(slots):
+        out[s] = (dense[s] + dot(back, e_bx[s])).astype(BF)
 
 
 def last_kernel(lv, slots, pack, dps, gr, split, pre, padded, e_up, kind, full, dw_one, dw_down, xcol):
@@ -398,51 +456,69 @@
     dw_one[...] = total_one.astype(BF)
 
 
-def reduce_kernel(n, dps, group, pack, one, down, two, o_one, o_down, o_two,
-                  packed, rs, acc, zb, fin, ms, mr, zs, zr, fs, fr):
+def reduce_kernel(n, dps, group, pack, one, down, two, out,
+                  packed, r0, a1, rs, acc, zb, fin, ps, pr, ms, mr, zs, zr, fs, fr, qs, qr):
     dp = lax.axis_index("dp")
-    mine, others = members(n, group)
-    me = lax.axis_index("space")
-    base = me - mine
+    core, chip, sibling, others, targets = members(n, group)
+    chips = group // 2
     peers = [lax.rem(dp + k, dps) for k in range(1, dps)]
     r1, r2 = pack.one[0], pack.rows
     for d in range(dps):
         pack.put(packed.at[d], one[d * r1 : (d + 1) * r1], down[d * r2 : (d + 1) * r2], two[d * r2 : (d + 1) * r2])
-    barrier([{"space": t} for t in others] + [{"dp": t} for t in peers])
-    lanes = pack.lanes(mine)
+    barrier([{"space": t} for t in targets + [sibling]] + [{"dp": t} for t in peers])
+    order = others + [chip]
     copies = []
-    for j, t in enumerate(others):
-        c = pltpu.make_async_remote_copy(
-            src_ref=packed.at[:, :, pack.lanes(t - base)], dst_ref=rs.at[j],
-            send_sem=ms.at[j], recv_sem=mr.at[j], device_id={"space": t}, device_id_type=MESH)
+    for j, t in enumerate(order):
+        c = remote(packed.at[:, :, pack.lanes((1 - core) * chips + t)], r0.at[j], ps.at[j], pr.at[j],
+                   {"space": sibling})
         c.start()
         copies.append(c)
-    total = packed[:, :, lanes].astype(F32)
-    for j, c in enumerate(copies):
-        c.wait()
-        total = total + rs[j].astype(F32)
-    acc[...] = total.astype(BF)
+    sent = []
+    for j, t in enumerate(order):
+        copies[j].wait()
+        value = packed[:, :, pack.lanes(core * chips + t)].astype(F32) + r0[j].astype(F32)
+        if j < chips - 1:
+            a1[j] = value.astype(BF)
+            c = remote(a1.at[j], rs.at[j], ms.at[j], mr.at[j], {"space": targets[j]})
+            c.start()
+            sent.append(c)
+    for j, c in enumerate(sent):
+        c.wait()
+        value = value + rs[j].astype(F32)
+    acc[...] = value.astype(BF)
     copies = []
     for j, t in enumerate(peers):
-        c = pltpu.make_async_remote_copy(
-            src_ref=acc.at[t], dst_ref=zb.at[j],
-            send_sem=zs.at[j], recv_sem=zr.at[j], device_id={"dp": t}, device_id_type=MESH)
+        c = remote(acc.at[t], zb.at[j], zs.at[j], zr.at[j], {"dp": t})
         c.start()
         copies.append(c)
     total = acc[dp].astype(F32)
     for j, c in enumerate(copies):
         c.wait()
         total = total + zb[j].astype(F32)
+    lanes = pack.lanes(core * chips + chip)
     fin[:, lanes] = total.astype(BF)
-    copies = []
-    for j, t in enumerate(others):
-        c = pltpu.make_async_remote_copy(
-            src_ref=fin.at[:, lanes], dst_ref=fin.at[:, lanes],
-            send_sem=fs.at[j], recv_sem=fr.at[j], device_id={"space": t}, device_id_type=MESH)
+    block = fin.at[:, lanes]
+    copies, last = [], []
+    for j, t in enumerate(targets):
+        c = remote(block, block, fs.at[j], fr.at[j], {"space": t})
         c.start()
         copies.append(c)
-    for c in copies:
-        c.wait()
+    c = remote(block, block, qs.at[chips - 1], qr.at[chips - 1], {"space": sibling})
+    c.start()
+    last.append(c)
+    for j, c in enumerate(copies):
+        c.wait()
+        block = fin.at[:, pack.lanes(core * chips + lax.rem(chip + chips - 1 - j, chips))]
+        c = remote(block, block, qs.at[j], qr.at[j], {"space": sibling})
+        c.start()
+        last.append(c)
+    for c in last:
+        c.wait()
+    out[...] = fin[...]
+
+
+def unfold_kernel(pack, fin, o_one, o_down, o_two):
+    r1 = pack.one[0]
     a = pack.at_one
     o_two[...] = fin[:, 0 : pack.at_down].astype(F32)
     o_down[...] = fin[:, pack.at_down : a].astype(F32)
@@ -465,6 +541,7 @@
 def on_device(features, cotangent, conv_one, down_weight, conv_two, patch_home, patch_links):
     n, dps = lax.axis_size("space"), lax.axis_size("dp")
     group = 8 if n % 8 == 0 else n
+    chips = group // 2
     slots, c1 = features.shape[1], features.shape[2]
     c2 = conv_two.shape[0] * dps
     me = lax.axis_index("space")
@@ -487,7 +564,8 @@
         [VM, SM, VM, VM, VM, VM, VM],
         [((slots, c1, 128), BF), ((slots, c1, 256), BF), ((dps, pack.rows, pack.total), BF)],
         [pltpu.VMEM((pack.rows, pack.total), BF), pltpu.VMEM((dps, pack.rows, pack.total), BF),
-         dma((dps - 1,)), dma((dps - 1,)), dma((dps - 1, group - 1)), dma((dps - 1, group - 1))]
+         dma((dps - 1,)), dma((dps - 1,)), dma((dps - 1, chips - 1)), dma((dps - 1, chips - 1)),
+         dma((dps - 1, chips)), dma((dps - 1, chips))]
         + halo_scratch(slots, c1),
         0,
     )
@@ -512,12 +590,64 @@
         [pltpu.VMEM((c1, conv_one.shape[1]), BF), pltpu.VMEM((27 * c1, one.out), BF)],
     )
 
+    sides = [(s, f) for s in range(slots) for f in range(2)]
+    last = two.xy - 1
+    place_of = {}
+    for i, (s, f) in enumerate(sides):
+        for k in range(two.z):
+            for y in range(two.xy):
+                place_of["x", s, f, y, k] = i * two.yz + y * two.z + k
+            for xe in range(two.xy + 2):
+                place_of["y", s, f, xe, k] = i * (two.xy + 2) * two.z + xe * two.z + k
+    send_x, send_y, rim_y = [], [], []
+    pad_x, pad_y, g_y, b_y, g_x, b_x = ([[] for s in range(slots)] for unused in range(6))
+    for (axis, s, f, a, k), lane in place_of.items():
+        inner = (0, last)[f]
+        rim = (two.xy, -1)[f]
+        far = (-1, two.xy)[f]
+        near_cell = (last, 0)[f]
+        if axis == "x":
+            send_x.append((s * two.cells + two.cell(inner, a, k), lane))
+            pad_x[s].append((lane, two.pad(rim, a, k)))
+            g_x[s].append((two.pad(far, a, k), lane))
+            b_x[s].append((lane, two.cell(near_cell, a, k)))
+            for g in range(2):
+                if a == (0, last)[g]:
+                    rim_y.append((lane, place_of["y", s, g, rim + 1, k]))
+        else:
+            if 0 < a <= two.xy:
+                send_y.append((s * two.cells + two.cell(a - 1, inner, k), lane))
+            pad_y[s].append((lane, two.pad(a - 1, rim, k)))
+            g_y[s].append((two.pad(a - 1, far, k), lane))
+            b_y[s].append((lane, two.pad(a - 1, near_cell, k)))
+
+    def stack(rows, cols, lists):
+        return jnp.stack([onehot(rows, cols, pairs) for pairs in lists])
+
+    def route(first, length):
+        lane = np.arange(128)
+        used = lane < 2 * slots * length
+        same = (lane % length)[:, None] == (lane % length)[None, :]
+        side = lane // length
+        same &= (side % 2)[:, None] == (side % 2)[None, :]
+        same &= used[:, None] & used[None, :]
+        slot = jnp.asarray(np.where(used, side // 2, 0), jnp.int32)
+        wanted = jnp.stack([source[:, first + 1], source[:, first]], axis=1)
+        wanted = jnp.broadcast_to(wanted[:, :, None], (slots, 2, length)).reshape(-1)
+        wanted = jnp.pad(wanted, (0, 128 - wanted.shape[0]), constant_values=-1)
+        base = (me - 2 + jnp.arange(5, dtype=jnp.int32)) * slots
+        hit = wanted[None, None, :] == base[:, None, None] + slot[None, :, None]
+        hit = hit & jnp.asarray(same)[None] & (wanted >= 0)[None, None, :]
+        return hit.astype(BF)
+
+    way_x, way_y = route(0, two.yz), route(2, (two.xy + 2) * two.z)
     rx2, ry2 = call(
         functools.partial(halo_kernel, n, two, slots),
-        (reduced, sel, two.face_y(), two.rim_to_face_y()),
-        [VM, SM, VM, VM],
-        [((slots, c2, 128), BF), ((slots, c2, 256), BF)],
-        halo_scratch(slots, c2),
+        (reduced, way_x, way_y, onehot(slots * cells_two, 128, send_x), onehot(slots * cells_two, 128, send_y),
+         onehot(128, 128, rim_y)),
+        [VM] * 6,
+        [((c2, 128), BF), ((c2, 128), BF)],
+        packed_scratch(c2),
         1,
     )
 
@@ -525,7 +655,8 @@
     trim = [(two.pos(*c), two.cell(*c)) for c in two.all()]
     level, dw_two, gp = call(
         functools.partial(second_kernel, two, slots, pack, dps, scale),
-        (reduced, rx2, ry2, two.place(), two.place_x(), two.place_y(), onehot(two.out, cells_two, trim),
+        (reduced, rx2, ry2, two.place(), stack(128, two.wide, pad_x), stack(128, two.wide, pad_y),
+         onehot(two.out, cells_two, trim),
          onehot(cells_two, two.out, [(b, a) for a, b in trim]), cotangent[0], live, full),
         [VM] * 9 + [SM, VM],
         [((slots, c2, cells_two), BF), ((c2, 27 * c2), BF), ((slots, c2, two.out), F32)],
@@ -533,25 +664,14 @@
          pltpu.VMEM((c2, 27 * c2), BF), pltpu.VMEM((3, c2, 256 + two.out), BF)],
     )
 
-    last = two.xy - 1
-    g_y, b_y, g_x, b_x = [], [], [], []
-    for k in range(two.z):
-        for xe in range(two.xy + 2):
-            lane = xe * two.z + k
-            g_y += [(two.pad(xe - 1, -1, k), lane), (two.pad(xe - 1, two.xy, k), 128 + lane)]
-            b_y += [(lane, two.pad(xe - 1, last, k)), (128 + lane, two.pad(xe - 1, 0, k))]
-        for y in range(two.xy):
-            lane = y * two.z + k
-            g_x += [(two.pad(-1, y, k), lane), (two.pad(two.xy, y, k), 64 + lane)]
-            b_x += [(lane, two.cell(last, y, k)), (64 + lane, two.cell(0, y, k))]
     dense = [(two.pad(*c), two.cell(*c)) for c in two.all()]
     [gr] = call(
-        functools.partial(back_kernel, n, two, slots),
-        (gp, sel, onehot(two.out, 256, g_y), onehot(256, two.out, b_y), onehot(two.out, 128, g_x),
-         onehot(two.out, cells_two, dense), onehot(128, cells_two, b_x)),
-        [VM, SM, VM, VM, VM, VM, VM],
+        functools.partial(back_kernel, n, slots),
+        (gp, way_x, way_y, stack(two.out, 128, g_y), stack(128, two.out, b_y), stack(two.out, 128, g_x),
+         onehot(two.out, cells_two, dense), stack(128, cells_two, b_x)),
+        [VM] * 8,
         [((slots, c2, cells_two), BF)],
-        halo_scratch(slots, c2),
+        packed_scratch(c2),
         2,
     )
 
@@ -563,16 +683,25 @@
         [pltpu.VMEM((27 * c1, one.out), BF)],
     )
 
-    outs = call(
+    part = (dps, pack.rows, pack.part)
+    [fin] = call(
         functools.partial(reduce_kernel, n, dps, group, pack),
         (dw_one, dw_down, dw_two),
         [VM] * 3,
+        [((pack.rows, pack.total), BF)],
+        [pltpu.VMEM((dps, pack.rows, pack.total), BF), pltpu.VMEM((chips,) + part, BF),
+         pltpu.VMEM((chips - 1,) + part, BF), pltpu.VMEM((chips - 1,) + part, BF),
+         pltpu.VMEM(part, BF), pltpu.VMEM((dps - 1, pack.rows, pack.part), BF),
+         pltpu.VMEM((pack.rows, pack.total), BF)]
+        + [dma((k,)) for k in (chips, chips, chips - 1, chips - 1, dps - 1, dps - 1, chips - 1, chips - 1, chips, chips)],
+        3,
+    )
+    outs = call(
+        functools.partial(unfold_kernel, pack),
+        (fin,),
+        [VM],
         [(conv_one.shape, F32), (down_weight.shape, F32), (conv_two.shape, F32)],
-        [pltpu.VMEM((dps, pack.rows, pack.total), BF), pltpu.VMEM((group - 1, dps, pack.rows, pack.part), BF),
-         pltpu.VMEM((dps, pack.rows, pack.part), BF), pltpu.VMEM((dps - 1, pack.rows, pack.part), BF),
-         pltpu.VMEM((pack.rows, pack.total), BF),
-         dma((group - 1,)), dma((group - 1,)), dma((dps - 1,)), dma((dps - 1,)), dma((group - 1,)), dma((group - 1,))],
-        3,
+        [],
     )
     if n > group:
         rings = [[a + m for a in range(0, n, group)] for m in range(group)]

time: 146 us -> 113 us (0.77)
  Pallas kernels: 136 us -> 104 us
  local copies, waits for them, and re-layouts: 5.69 us -> 1.26 us
  other arithmetic: 3.16 us -> 5.76 us
    pallas_call x7 -> x8, Pallas kernels: 136 us -> 104 us  [call(): pl.pallas_call(body, out_shape=[jax.ShapeDtypeStruct(s, t) for s, t in ou...]
    unnamed x3 -> x0, local copies, waits for them, and re-layouts: 4.83 us -> none
    convert_element_type x0 -> x1, other arithmetic: none -> 1.72 us  [route(): return hit.astype(BF)]
where the time goes in v2:
time: 113 us; the launch traced here: 112 us
  Pallas kernels  104 us (92%)
  other arithmetic  5.76 us (5%)
  local copies, waits for them, and re-layouts  1.26 us (1%)
    pallas_call x8, Pallas kernels, call(): pl.pallas_call(body, out_shape=[jax.ShapeDtypeStruct(s, t) for s, t in ou...  104 us

profile of v2, /device:TPU:0, one launch (start us, length us, event | category | flops | bytes accessed | tf_op | source)
XLA Modules:
  0.0 112.2 jit_solution(10724990756951187384)
XLA Ops:
  0.7 0.8 fusion
  1.5 0.5 convert_element_type.20.live
  2.0 0.8 select_reduce_fusion.1
  2.8 0.9 select_reduce_fusion
  3.7 0.1 copy.55
  3.8 0.1 copy.54
  3.9 0.1 and_convert_fusion.2
  4.0 0.7 reshape.136.sel
  4.7 0.7 broadcast_add_fusion
  5.5 0.1 pad_add_fusion.1
  5.6 0.1 broadcast_in_dim.40
  5.6 0.1 reshape.135
  5.7 0.1 pad_add_fusion
  5.8 0.1 broadcast_in_dim.39
  5.9 0.1 reshape.134
  6.0 1.7 %and_convert_fusion = (bf16[5,128,128]{2,1,0:T(8,128)(2,1)}, bf16[5,128,128]{2,1,0:T(8,128)(2,1)}) fusion(s32[5,128]{1,0:T(8,128)S(1)} %get-tuple-element.44, s32[128]{0:T(128)S(1)} %pad.9, pred[128]{0:T(512)(128)(4,1)S(1)} %broadcast_compare_fusion.2, pred[128,128]{1,0:T(8,128)(4,1)} %bitcast.11, pred[128]{0:T(512)(128)(4,1)S(1)} %broadcast_compare_fusion.3, ...), kind=kLoop, calls=%fused_computation | loop fusion | flops 655360 | bytes 366848 | tf_op jit(solution)/shard_map/convert_element_type | solution.py:641
  7.7 26.6 %shard_map.435 = (bf16[3,64,128]{2,1,0:T(8,128)(2,1)}, bf16[3,64,256]{2,1,0:T(8,128)(2,1)}, bf16[4,32,5120]{2,1,0:T(8,128)(2,1)}) custom-call(bf16[3,64,1024]{2,1,0:T(8,128)(2,1)} %bitcast.7, f32[180]{0:T(256)} %reshape.136.sel, bf16[1024,256]{1,0:T(8,128)(2,1)} %constant.43.clone.e_face, bf16[128,256]{1,0:T(8,128)(2,1)} %constant.94.clone.e_rim, ...), custom_call_target="tpu_custom_call" | custom-call | tf_op jit(solution)/shard_map/pallas_call | solution.py:531
  34.3 9.7 %shard_map.436 = (bf16[3,64,1408]{2,1,0:T(8,128)(2,1)}, f32[3,64,1152]{2,1,0:T(8,128)}, bf16[3,512,128]{2,1,0:T(8,128)(2,1)}, bf16[3,128,128]{2,1,0:T(8,128)(2,1)}) custom-call(bf16[3,64,1024]{2,1,0:T(8,128)(2,1)} %bitcast.8, bf16[3,64,128]{2,1,0:T(8,128)(2,1)} %get-tuple-element.21.rx, bf16[3,64,256]{2,1,0:T(8,128)(2,1)} %get-tuple-element.22.ry, ...), custom_call_target="tpu_custom_call" | custom-call | tf_op jit(solution)/shard_map/pallas_call | solution.py:531
  44.0 11.8 %shard_map.437 = (bf16[128,128]{1,0:T(8,128)(2,1)}, bf16[128,128]{1,0:T(8,128)(2,1)}) custom-call(bf16[3,128,128]{2,1,0:T(8,128)(2,1)} %get-tuple-element.24.field, bf16[5,128,128]{2,1,0:T(8,128)(2,1)} %get-tuple-element.47.way_x, bf16[5,128,128]{2,1,0:T(8,128)(2,1)} %get-tuple-element.46.way_y, bf16[384,128]{1,0:T(8,128)(2,1)} %constant.103.clone.e_x, ...), custom_call_target="tpu_custom_call" | custom-call | tf_op jit(solution)/shard_map/pallas_call | solution.py:531
  55.8 10.9 %shard_map.438 = (bf16[3,128,128]{2,1,0:T(8,128)(2,1)}, bf16[128,3456]{1,0:T(8,128)(2,1)}, f32[3,128,256]{2,1,0:T(8,128)}) custom-call(bf16[3,128,128]{2,1,0:T(8,128)(2,1)} %get-tuple-element.24.field, bf16[128,128]{1,0:T(8,128)(2,1)} %get-tuple-element.25.rx, bf16[128,128]{1,0:T(8,128)(2,1)} %get-tuple-element.26.ry, ...), custom_call_target="tpu_custom_call" | custom-call | tf_op jit(solution)/shard_map/pallas_call | solution.py:531
  66.7 11.0 %shard_map.439.gr = bf16[3,128,128]{2,1,0:T(8,128)(2,1)} custom-call(f32[3,128,256]{2,1,0:T(8,128)} %get-tuple-element.28.gp, bf16[5,128,128]{2,1,0:T(8,128)(2,1)} %get-tuple-element.47.way_x, bf16[5,128,128]{2,1,0:T(8,128)(2,1)} %get-tuple-element.46.way_y, bf16[3,256,128]{2,1,0:T(8,128)(2,1)} %constant.147.e_gy, bf16[3,128,256]{2,1,0:T(8,128)(2,1)} %constant.151.e_by, ...), custom_call_target="tpu_custom_call" | custom-call | tf_op jit(solution)/shard_map/pallas_call | solution.py:531
  77.8 8.5 %shard_map.440 = (bf16[64,1728]{1,0:T(8,128)(2,1)}, bf16[128,512]{1,0:T(8,128)(2,1)}) custom-call(bf16[3,128,128]{2,1,0:T(8,128)(2,1)} %shard_map.439.gr, bf16[3,512,128]{2,1,0:T(8,128)(2,1)} %get-tuple-element.29.split, f32[3,64,1152]{2,1,0:T(8,128)} %get-tuple-element.30.pre, bf16[3,64,1408]{2,1,0:T(8,128)(2,1)} %get-tuple-element.31.padded, ...), custom_call_target="tpu_custom_call" | custom-call | tf_op jit(solution)/shard_map/pallas_call | solution.py:531
  86.3 24.1 %shard_map.441.fin = bf16[32,5120]{1,0:T(8,128)(2,1)} custom-call(bf16[64,1728]{1,0:T(8,128)(2,1)} %get-tuple-element.32.one, bf16[128,512]{1,0:T(8,128)(2,1)} %get-tuple-element.33.down, bf16[128,3456]{1,0:T(8,128)(2,1)} %get-tuple-element.34.two), custom_call_target="tpu_custom_call" | custom-call | tf_op jit(solution)/shard_map/pallas_call | solution.py:531
  110.4 1.8 %shard_map.442 = (f32[16,1728]{1,0:T(8,128)}, f32[32,512]{1,0:T(8,128)}, f32[32,3456]{1,0:T(8,128)}) custom-call(bf16[32,5120]{1,0:T(8,128)(2,1)} %shard_map.441.fin), custom_call_target="tpu_custom_call" | custom-call | tf_op jit(solution)/shard_map/pallas_call | solution.py:531
  (9 shorter events, 0.1 us)

commit v3 on v2

--- a/solution.py
+++ b/solution.py
@@ -165,13 +165,14 @@
     return result
 
 
-def halo_body(n, lv, slots, field, sel, e_face, e_rim, rx, ry, sx, sy, gx, gy, xs, xr, ys, yr, between):
+def halo_body(n, lv, slots, field, sel, e_face, e_rim, rx, ry, sx, sy, gx, gy, xs, xr, ys, yr, early, between):
     chan = field.shape[1]
     last = lv.cells - lv.yz
     sx[...] = jnp.zeros_like(sx)
     sx[:, :, 0 : lv.yz] = field[:, :, 0 : lv.yz]
     sx[:, :, 64 : 64 + lv.yz] = field[:, :, last : lv.cells]
     order, copies = swap(n, sx, gx, 1, xs, xr)
+    early()
     base = dot(field[...].reshape(slots * chan, lv.cells), e_face[...])
     for c in copies:
         c.wait()
@@ -241,36 +242,37 @@
     barrier([{"space": t} for t in near(n).values()] + [{"space": t} for t in targets + [sibling]]
             + [{"dp": t} for t in peers])
     lanes = pack.lanes(core * chips + chip)
-    zc = []
+    zc, mc, sc = [], [], []
     for i, t in enumerate(peers):
         zc.append(remote(packed.at[:, lanes], gath.at[dp, :, lanes], zs.at[i], zr.at[i], {"dp": t}))
-    for c in zc:
-        c.start()
-    gath[dp] = packed[...]
-    mc, sc = [], []
     shares = [lax.rem(dp + dps - 1 - i, dps) for i in range(dps - 1)]
-    for i in range(dps - 1):
-        zc[i].wait()
-        block = gath.at[shares[i], :, lanes]
-        for j, t in enumerate(targets):
-            c = remote(block, block, ms.at[i, j], mr.at[i, j], {"space": t})
+
+    def early():
+        for c in zc:
             c.start()
-            mc.append(c)
-        c = remote(block, block, ps.at[i, chips - 1], pr.at[i, chips - 1], {"space": sibling})
-        c.start()
-        sc.append(c)
+        gath[dp] = packed[...]
 
     def between():
         for i in range(dps - 1):
-            for j in range(chips - 1):
-                mc[i * (chips - 1) + j].wait()
-                sender = lax.rem(chip + chips - 1 - j, chips)
-                block = gath.at[shares[i], :, pack.lanes(core * chips + sender)]
-                c = remote(block, block, ps.at[i, j], pr.at[i, j], {"space": sibling})
+            zc[i].wait()
+            block = gath.at[shares[i], :, lanes]
+            for j, t in enumerate(targets):
+                c = remote(block, block, ms.at[i, j], mr.at[i, j], {"space": t})
                 c.start()
-                sc.append(c)
-
-    halo_body(n, lv, slots, field, sel, e_face, e_rim, rx, ry, *halo, between)
+                mc.append(c)
+            c = remote(block, block, ps.at[i, chips - 1], pr.at[i, chips - 1], {"space": sibling})
+            c.start()
+            sc.append(c)
+
+    halo_body(n, lv, slots, field, sel, e_face, e_rim, rx, ry, *halo, early, between)
+    for i in range(dps - 1):
+        for j in range(chips - 1):
+            mc[i * (chips - 1) + j].wait()
+            sender = lax.rem(chip + chips - 1 - j, chips)
+            block = gath.at[shares[i], :, pack.lanes(core * chips + sender)]
+            c = remote(block, block, ps.at[i, j], pr.at[i, j], {"space": sibling})
+            c.start()
+            sc.append(c)
     for c in sc:
         c.wait()
     full[...] = gath[...]
@@ -526,6 +528,45 @@
     o_one[:, pack.half :] = fin[r1 : 2 * r1, a : a + pack.rest].astype(F32)
 
 
+def table_kernel(slots, home, links, same_x, same_y, sel, live, way_x, way_y, src):
+    me = lax.axis_index("space")
+    for s in range(slots):
+        live[s] = jnp.float32(0.0)
+        for f in range(4):
+            src[s * 4 + f] = jnp.int32(-1)
+
+    @pl.loop(0, home.shape[0])
+    def _(p):
+        slot = home[p] - me * slots
+
+        @pl.when((slot >= 0) & (slot < slots))
+        def _():
+            live[slot] = jnp.float32(1.0)
+            for f in range(4):
+                q = links[p * 4 + f]
+                src[slot * 4 + f] = jnp.where(q >= 0, home[jnp.maximum(q, 0)], -1)
+
+    for f in range(4):
+        for s in range(slots):
+            code = src[s * 4 + f]
+            for k in range(5):
+                for t in range(slots):
+                    hit = (code >= 0) & (code == (me + k - 2) * slots + t)
+                    sel[((f * slots + s) * 5 + k) * slots + t] = jnp.where(hit, jnp.float32(1.0), jnp.float32(0.0))
+    for way, same, first in ((way_x, same_x, 0), (way_y, same_y, 2)):
+        width = same.shape[2]
+        group = same[1]
+        wanted = jnp.full((width, width), -1, jnp.int32)
+        for s in range(slots):
+            for f in range(2):
+                wanted = jnp.where(group == 2 * s + f, src[s * 4 + first + 1 - f], wanted)
+        slot = same[0]
+        meets = (slot >= 0) & (wanted >= 0)
+        for k in range(5):
+            hit = meets & (wanted == slot + (me + k - 2) * slots)
+            way[k] = jnp.where(hit, 1.0, 0.0).astype(BF)
+
+
 def call(body, args, specs, outs, scratch, ident=None):
     extra = {} if ident is None else {"collective_id": ident, "has_side_effects": True}
     return pl.pallas_call(
@@ -544,17 +585,28 @@
     chips = group // 2
     slots, c1 = features.shape[1], features.shape[2]
     c2 = conv_two.shape[0] * dps
-    me = lax.axis_index("space")
     one, two = Level(PXY, PZ), Level(PXY // 2, PZ // 2)
     pack = Pack(conv_one.shape, down_weight.shape, conv_two.shape, group)
 
-    own = patch_home[None, :] == (me * slots + jnp.arange(slots, dtype=jnp.int32))[:, None]
-    live = jnp.any(own, axis=1).astype(F32)
-    ids = jnp.arange(patch_home.shape[0], dtype=jnp.int32)
-    codes = (me - 2) * slots + jnp.arange(5 * slots, dtype=jnp.int32)
-    target = jnp.max(jnp.where(own[:, :, None], patch_links[None], -1), axis=1)
-    source = jnp.max(jnp.where(target[:, :, None] == ids, patch_home, -1), axis=2)
-    sel = ((source.T[:, :, None] == codes) & (source.T[:, :, None] >= 0)).astype(F32).reshape(-1)
+    def meeting(length):
+        lane = np.arange(128)
+        used = lane < 2 * slots * length
+        same = (lane % length)[:, None] == (lane % length)[None, :]
+        side = lane // length
+        same &= (side % 2)[:, None] == (side % 2)[None, :]
+        same &= used[:, None] & used[None, :]
+        slot = np.where(same, (side // 2)[:, None], -1)
+        group_of = np.where(same, side[None, :], -1)
+        return jnp.asarray(np.stack([slot, group_of]), jnp.int32)
+
+    sel, live, way_x, way_y = pl.pallas_call(
+        functools.partial(table_kernel, slots),
+        out_shape=[jax.ShapeDtypeStruct((20 * slots * slots,), F32), jax.ShapeDtypeStruct((slots,), F32),
+                   jax.ShapeDtypeStruct((5, 128, 128), BF), jax.ShapeDtypeStruct((5, 128, 128), BF)],
+        in_specs=[SM, SM, VM, VM],
+        out_specs=[SM, SM, VM, VM],
+        scratch_shapes=[pltpu.SMEM((4 * slots,), jnp.int32)],
+    )(patch_home, patch_links.reshape(-1), meeting(two.yz), meeting((two.xy + 2) * two.z))
 
     field = features[0]
     dma = pltpu.SemaphoreType.DMA
@@ -624,23 +676,6 @@
     def stack(rows, cols, lists):
         return jnp.stack([onehot(rows, cols, pairs) for pairs in lists])
 
-    def route(first, length):
-        lane = np.arange(128)
-        used = lane < 2 * slots * length
-        same = (lane % length)[:, None] == (lane % length)[None, :]
-        side = lane // length
-        same &= (side % 2)[:, None] == (side % 2)[None, :]
-        same &= used[:, None] & used[None, :]
-        slot = jnp.asarray(np.where(used, side // 2, 0), jnp.int32)
-        wanted = jnp.stack([source[:, first + 1], source[:, first]], axis=1)
-        wanted = jnp.broadcast_to(wanted[:, :, None], (slots, 2, length)).reshape(-1)
-        wanted = jnp.pad(wanted, (0, 128 - wanted.shape[0]), constant_values=-1)
-        base = (me - 2 + jnp.arange(5, dtype=jnp.int32)) * slots
-        hit = wanted[None, None, :] == base[:, None, None] + slot[None, :, None]
-        hit = hit & jnp.asarray(same)[None] & (wanted >= 0)[None, None, :]
-        return hit.astype(BF)
-
-    way_x, way_y = route(0, two.yz), route(2, (two.xy + 2) * two.z)
     rx2, ry2 = call(
         functools.partial(halo_kernel, n, two, slots),
         (reduced, way_x, way_y, onehot(slots * cells_two, 128, send_x), onehot(slots * cells_two, 128, send_y),

time: 113 us -> 108 us (0.956)
  other arithmetic: 5.76 us -> 0 us
  Pallas kernels: 104 us -> 106 us
    pallas_call x0 -> x1, Pallas kernels: none -> 2.48 us  [on_device(): pl.pallas_call(functools.partial(table_kernel, slots), out_shape=[jax.Sha...]
    convert_element_type x3 -> x0, other arithmetic: 2.29 us -> none  [the longest x1 1.72 us: route(): return hit.astype(BF)]
    reduce_max x2 -> x0, other arithmetic: 1.7 us -> none  [the longest x1 0.87 us: on_device(): jnp.max(jnp.where(target[:, :, None] == ids, patch_home, -1), axis=2)]
where the time goes in v3:
time: 108 us
  Pallas kernels  106 us (98%)
  local copies, waits for them, and re-layouts  1.36 us (1%)
    pallas_call x8, Pallas kernels, call(): pl.pallas_call(body, out_shape=[jax.ShapeDtypeStruct(s, t) for s, t in ou...  103 us
    pallas_call x1, Pallas kernels, on_device(): pl.pallas_call(functools.partial(table_kernel, slots), out_shape=[jax.Sha...  2.48 us

profile of v3, /device:TPU:0, one launch (start us, length us, event | category | flops | bytes accessed | tf_op | source)
XLA Modules:
  0.0 108.0 jit_solution(10608955538968298296)
XLA Ops:
  0.6 0.8 copy.47
  1.4 0.6 reshape.11.links
  2.0 2.5 %shard_map.417 = (f32[180]{0:T(256)}, f32[3]{0:T(128)}, bf16[5,128,128]{2,1,0:T(8,128)(2,1)}, bf16[5,128,128]{2,1,0:T(8,128)(2,1)}) custom-call(s32[16]{0:T(128)} %home.1, s32[64]{0:T(128)} %reshape.11.links, s32[2,128,128]{2,1,0:T(8,128)} %constant.70.clone.same_x, s32[2,128,128]{2,1,0:T(8,128)} %constant.71.clone.same_y), custom_call_target="tpu_custom_call" | custom-call | tf_op jit(solution)/shard_map/pallas_call | solution.py:602
  4.5 25.6 %shard_map.418 = (bf16[3,64,128]{2,1,0:T(8,128)(2,1)}, bf16[3,64,256]{2,1,0:T(8,128)(2,1)}, bf16[4,32,5120]{2,1,0:T(8,128)(2,1)}) custom-call(bf16[3,64,1024]{2,1,0:T(8,128)(2,1)} %bitcast.3, f32[180]{0:T(256)} %get-tuple-element.25.sel, bf16[1024,256]{1,0:T(8,128)(2,1)} %constant.72.clone.e_face, bf16[128,256]{1,0:T(8,128)(2,1)} %constant.73.clone.e_rim, ...), custom_call_target="tpu_custom_call" | custom-call | tf_op jit(solution)/shard_map/pallas_call | solution.py:572
  30.1 9.7 %shard_map.419 = (bf16[3,64,1408]{2,1,0:T(8,128)(2,1)}, f32[3,64,1152]{2,1,0:T(8,128)}, bf16[3,512,128]{2,1,0:T(8,128)(2,1)}, bf16[3,128,128]{2,1,0:T(8,128)(2,1)}) custom-call(bf16[3,64,1024]{2,1,0:T(8,128)(2,1)} %bitcast.4, bf16[3,64,128]{2,1,0:T(8,128)(2,1)} %get-tuple-element.26.rx, bf16[3,64,256]{2,1,0:T(8,128)(2,1)} %get-tuple-element.27.ry, ...), custom_call_target="tpu_custom_call" | custom-call | tf_op jit(solution)/shard_map/pallas_call | solution.py:572
  39.8 11.9 %shard_map.420 = (bf16[128,128]{1,0:T(8,128)(2,1)}, bf16[128,128]{1,0:T(8,128)(2,1)}) custom-call(bf16[3,128,128]{2,1,0:T(8,128)(2,1)} %get-tuple-element.29.field, bf16[5,128,128]{2,1,0:T(8,128)(2,1)} %get-tuple-element.30.way_x, bf16[5,128,128]{2,1,0:T(8,128)(2,1)} %get-tuple-element.31.way_y, bf16[384,128]{1,0:T(8,128)(2,1)} %constant.78.clone.e_x, ...), custom_call_target="tpu_custom_call" | custom-call | tf_op jit(solution)/shard_map/pallas_call | solution.py:572
  51.7 10.9 %shard_map.421 = (bf16[3,128,128]{2,1,0:T(8,128)(2,1)}, bf16[128,3456]{1,0:T(8,128)(2,1)}, f32[3,128,256]{2,1,0:T(8,128)}) custom-call(bf16[3,128,128]{2,1,0:T(8,128)(2,1)} %get-tuple-element.29.field, bf16[128,128]{1,0:T(8,128)(2,1)} %get-tuple-element.32.rx, bf16[128,128]{1,0:T(8,128)(2,1)} %get-tuple-element.33.ry, ...), custom_call_target="tpu_custom_call" | custom-call | tf_op jit(solution)/shard_map/pallas_call | solution.py:572
  62.6 10.7 %shard_map.422.gr = bf16[3,128,128]{2,1,0:T(8,128)(2,1)} custom-call(f32[3,128,256]{2,1,0:T(8,128)} %get-tuple-element.36.gp, bf16[5,128,128]{2,1,0:T(8,128)(2,1)} %get-tuple-element.30.way_x, bf16[5,128,128]{2,1,0:T(8,128)(2,1)} %get-tuple-element.31.way_y, bf16[3,256,128]{2,1,0:T(8,128)(2,1)} %constant.118.e_gy, bf16[3,128,256]{2,1,0:T(8,128)(2,1)} %constant.122.e_by, ...), custom_call_target="tpu_custom_call" | custom-call | tf_op jit(solution)/shard_map/pallas_call | solution.py:572
  73.3 8.5 %shard_map.423 = (bf16[64,1728]{1,0:T(8,128)(2,1)}, bf16[128,512]{1,0:T(8,128)(2,1)}) custom-call(bf16[3,128,128]{2,1,0:T(8,128)(2,1)} %shard_map.422.gr, bf16[3,512,128]{2,1,0:T(8,128)(2,1)} %get-tuple-element.37.split, f32[3,64,1152]{2,1,0:T(8,128)} %get-tuple-element.38.pre, bf16[3,64,1408]{2,1,0:T(8,128)(2,1)} %get-tuple-element.39.padded, ...), custom_call_target="tpu_custom_call" | custom-call | tf_op jit(solution)/shard_map/pallas_call | solution.py:572
  81.8 24.3 %shard_map.424.fin = bf16[32,5120]{1,0:T(8,128)(2,1)} custom-call(bf16[64,1728]{1,0:T(8,128)(2,1)} %get-tuple-element.40.one, bf16[128,512]{1,0:T(8,128)(2,1)} %get-tuple-element.41.down, bf16[128,3456]{1,0:T(8,128)(2,1)} %get-tuple-element.42.two), custom_call_target="tpu_custom_call" | custom-call | tf_op jit(solution)/shard_map/pallas_call | solution.py:572
  106.2 1.8 %shard_map.425 = (f32[16,1728]{1,0:T(8,128)}, f32[32,512]{1,0:T(8,128)}, f32[32,3456]{1,0:T(8,128)}) custom-call(bf16[32,5120]{1,0:T(8,128)(2,1)} %shard_map.424.fin), custom_call_target="tpu_custom_call" | custom-call | tf_op jit(solution)/shard_map/pallas_call | solution.py:572
